TPU v7x, 32 devices: a whole 2x2x4 slice. The times are simulated.
32 devices in a mesh: rows: 16 (over z, y, core), seq: 2 (over x).
Axes of the slice: x: 2, y: 2, z: 4, core: 2. Of those that a mesh axis runs over, the one named last changes fastest.
Arguments:
- hidden_in: bfloat16 [16, 1280, 512], P('rows', 'seq'), may hold values from -6 to 6
- memory: bfloat16 [16, 256, 512], P('rows', 'seq'), may hold values from -6 to 6
- grad_out: bfloat16 [16, 1280, 512], P('rows', 'seq'), may hold values from -6 to 6
- seg_ids: int32 [16, 1280], P('rows'), may hold values from 0 to 2, as said below
- mem_seg_ids: int32 [16, 256], P('rows'), may hold values from 0 to 2, as said below
- gains: bfloat16 [5, 512], P(None, 'seq'), may hold values from 0.25 to 1.75
- qkv_first: bfloat16 [512, 1536], P('seq'), may hold values from -0.25 to 0.25
- query_cross: bfloat16 [512, 512], P('seq'), may hold values from -0.25 to 0.25
- kv_cross: bfloat16 [512, 1024], P('seq'), may hold values from -0.25 to 0.25
- out_first: bfloat16 [1024, 512], P(None, 'seq'), may hold values from -2 to 2
- taps_left: bfloat16 [11, 512], P(None, 'seq'), may hold values from -1.75 to 1.75
- proj_left: bfloat16 [512, 1024], P('seq'), may hold values from -0.25 to 0.25
- taps_right: bfloat16 [7, 512], P(None, 'seq'), may hold values from -2 to 2
- proj_right: bfloat16 [512, 256], P('seq'), may hold values from -0.25 to 0.25
- mid_gain: bfloat16 [1024], P('seq'), may hold values from 0.25 to 1.75
- taps_mid: bfloat16 [7, 1024], P(None, 'seq'), may hold values from -2 to 2
- proj_mid: bfloat16 [1024, 512], P(None, 'seq'), may hold values from -0.375 to 0.375
- qkv_second: bfloat16 [512, 1536], P('seq'), may hold values from -0.25 to 0.25
- out_second: bfloat16 [512, 512], P('seq'), may hold values from -2 to 2
- query_last: bfloat16 [512, 512], P('seq'), may hold values from -0.25 to 0.25
- kv_last: bfloat16 [512, 1024], P('seq'), may hold values from -0.25 to 0.25
- out_last: bfloat16 [512, 512], P('seq'), may hold values from -2 to 2
- ffn_up: bfloat16 [512, 2048], P('seq'), may hold values from -0.25 to 0.25
- ffn_down: bfloat16 [2048, 512], P(None, 'seq'), may hold values from -0.125 to 0.125
Outputs:
- output: bfloat16 [16, 1280, 512], P('rows', 'seq')
- grad_in: float32 [16, 1280, 512], P('rows', 'seq')
- grad_mem: float32 [16, 256, 512], P('rows', 'seq')
- grad_gains: float32 [5, 512], P(None, 'seq')
- grad_qkv_first: float32 [512, 1536], P('seq')
- grad_query_cross: float32 [512, 512], P('seq')
- grad_kv_cross: float32 [512, 1024], P('seq')
- grad_out_first: float32 [1024, 512], P(None, 'seq')
- grad_taps_left: float32 [11, 512], P(None, 'seq')
- grad_proj_left: float32 [512, 1024], P('seq')
- grad_taps_right: float32 [7, 512], P(None, 'seq')
- grad_proj_right: float32 [512, 256], P('seq')
- grad_mid_gain: float32 [1024], P('seq')
- grad_taps_mid: float32 [7, 1024], P(None, 'seq')
- grad_proj_mid: float32 [1024, 512], P(None, 'seq')
- grad_qkv_second: float32 [512, 1536], P('seq')
- grad_out_second: float32 [512, 512], P('seq')
- grad_query_last: float32 [512, 512], P('seq')
- grad_kv_last: float32 [512, 1024], P('seq')
- grad_out_last: float32 [512, 512], P('seq')
- grad_ffn_up: float32 [512, 2048], P('seq')
- grad_ffn_down: float32 [2048, 512], P(None, 'seq')
Inputs may be any that keep to these rules, and one draw needn't show every extreme that they name: `seg_ids`: in every row the ids never fall along the positions, and 0, 1 and 2 each occur. `mem_seg_ids`: in every row the ids never fall along the positions, and 0, 1 and 2 each occur.
All inputs are finite; a program needn't handle non-finite values.
Results may differ from a plain program's by a relative error of at most 0.02.
Values may be sent and summed in bfloat16 or wider, within the bound.
A program may use at most 320 MiB of HBM per device.

v0:
```python
import jax
import jax.numpy as jnp
from jax import lax
from jax.sharding import PartitionSpec as P

H_SELF = 16
H_CROSS = 8
WIDE = 1024
NARROW = 256
LEFT_TAPS = 11
RIGHT_TAPS = 7


NEG_BIG = -1e30
EPSILON = 1e-06
HIGH = lax.Precision.HIGHEST


def passed_along(block, axis, distance):
    devices = range(lax.axis_size(axis))
    route = [(i - distance, i) for i in devices if i - distance in devices]
    return lax.ppermute(block, axis, route)


def layer_norm(values, gain_vec):
    centre = values - jnp.mean(values, axis=-1, keepdims=True)
    inverse = lax.rsqrt(jnp.mean(centre * centre, axis=-1, keepdims=True) + EPSILON)
    return centre * inverse * gain_vec


def norm_back(values, gain_vec, upstream):
    centre = values - jnp.mean(values, axis=-1, keepdims=True)
    inverse = lax.rsqrt(jnp.mean(centre * centre, axis=-1, keepdims=True) + EPSILON)
    normed = centre * inverse
    scaled = upstream * gain_vec
    d_values = inverse * (
        scaled
        - jnp.mean(scaled, axis=-1, keepdims=True)
        - normed * jnp.mean(scaled * normed, axis=-1, keepdims=True)
    )
    return (d_values, jnp.sum(upstream * normed, axis=0))


def swish_slope(pre_act):
    sigma = jax.nn.sigmoid(pre_act)
    return sigma * (1.0 + pre_act * (1.0 - sigma))


def plain_dot(first, second):
    return jnp.dot(first, second, preferred_element_type=jnp.float32)


def left_dot(first, second):
    return jnp.einsum("nk,nm->km", first, second, preferred_element_type=jnp.float32)


def right_dot(grads_in, weight):
    return jnp.einsum("nm,km->nk", grads_in, weight, preferred_element_type=jnp.float32)


def conv_forward(extended, ext_seg, own_seg, tap_weights, rim_len):
    tok_count = own_seg.shape[0]
    result_sum = jnp.zeros((tok_count, extended.shape[1]), jnp.float32)
    for offset in range(tap_weights.shape[0]):
        lower = rim_len - offset
        window_rows = extended[lower : lower + tok_count]
        same_seg = (ext_seg[lower : lower + tok_count] == own_seg)[:, None]
        result_sum = result_sum + jnp.where(same_seg, window_rows, 0.0) * tap_weights[offset]
    return result_sum


def conv_back(grad_ext, grad_seg, own_seg, extended, ext_seg, tap_weights, rim_len):
    tok_count = own_seg.shape[0]
    d_input = jnp.zeros((tok_count, grad_ext.shape[1]), jnp.float32)
    local_grad = grad_ext[:tok_count]
    tap_grads = []
    for offset in range(tap_weights.shape[0]):
        later = grad_ext[offset : offset + tok_count]
        same_later = (grad_seg[offset : offset + tok_count] == own_seg)[:, None]
        d_input = d_input + jnp.where(same_later, later, 0.0) * tap_weights[offset]
        lower = rim_len - offset
        window_rows = extended[lower : lower + tok_count]
        same_seg = (ext_seg[lower : lower + tok_count] == own_seg)[:, None]
        tap_grads.append(jnp.sum(local_grad * jnp.where(same_seg, window_rows, 0.0), axis=0))
    return (d_input, jnp.stack(tap_grads, 0))


def key_scores(query_heads, key_block, kseg_block, kpos_block, own_seg, positions, causal):
    head_count = query_heads.shape[1]
    head_size = query_heads.shape[2]
    key_heads = key_block.reshape(key_block.shape[0], head_count, head_size)
    scores = jnp.einsum(
        "qhd,khd->hqk", query_heads, key_heads, preferred_element_type=jnp.float32
    ) * head_size ** (-0.5)
    allowed = kseg_block[None, :] == own_seg[:, None]
    if causal:
        allowed = jnp.logical_and(allowed, kpos_block[None, :] <= positions[:, None])
    return jnp.where(allowed[None], scores, NEG_BIG)


def key_blocks(keys, values, key_seg, pieces):
    total_keys = keys.shape[0]
    block_len = total_keys // pieces
    return (
        keys.reshape(pieces, block_len, keys.shape[1]),
        values.reshape(pieces, block_len, values.shape[1]),
        key_seg.reshape(pieces, block_len),
        jnp.arange(total_keys, dtype=jnp.int32).reshape(pieces, block_len),
    )


def attend_forward(queries, keys, values, head_count, own_seg, positions, key_seg, causal, pieces):
    tok_count, model_width = queries.shape
    head_size = model_width // head_count
    query_heads = queries.reshape(tok_count, head_count, head_size)
    blocked = key_blocks(keys, values, key_seg, pieces)

    def running(state_now, block_data):
        row_max, summed = state_now
        scores = key_scores(
            query_heads, block_data[0], block_data[2], block_data[3], own_seg, positions, causal
        )
        new_max = jnp.maximum(row_max, jnp.max(scores, axis=-1))
        summed = summed * jnp.exp(row_max - new_max) + jnp.sum(
            jnp.exp(scores - new_max[..., None]), axis=-1
        )
        return ((new_max, summed), None)

    start_state = (
        jnp.full((head_count, tok_count), NEG_BIG, jnp.float32),
        jnp.zeros((head_count, tok_count), jnp.float32),
    )
    (row_max, summed), _ = lax.scan(running, start_state, blocked)
    log_total = row_max + jnp.log(summed)

    def weighted(accumulated, block_data):
        scores = key_scores(
            query_heads, block_data[0], block_data[2], block_data[3], own_seg, positions, causal
        )
        weights_low = jnp.exp(scores - log_total[..., None]).astype(jnp.bfloat16)
        value_heads = block_data[1].reshape(block_data[1].shape[0], head_count, head_size)
        return (
            accumulated
            + jnp.einsum(
                "hqk,khd->qhd", weights_low, value_heads, preferred_element_type=jnp.float32
            ),
            None,
        )

    accumulated, _ = lax.scan(
        weighted, jnp.zeros((tok_count, head_count, head_size), jnp.float32), blocked
    )
    return (accumulated.reshape(tok_count, model_width), log_total)


def attend_back(
    queries,
    keys,
    values,
    grad_att,
    att_out,
    log_total,
    head_count,
    own_seg,
    positions,
    key_seg,
    causal,
    pieces,
):
    tok_count, model_width = queries.shape
    head_size = model_width // head_count
    query_heads = queries.reshape(tok_count, head_count, head_size)
    grad_heads = grad_att.reshape(tok_count, head_count, head_size)
    row_delta = jnp.sum(
        grad_att.astype(jnp.float32).reshape(tok_count, head_count, head_size)
        * att_out.reshape(tok_count, head_count, head_size),
        axis=-1,
    ).T
    blocked = key_blocks(keys, values, key_seg, pieces)

    def step_back(d_query, block_data):
        scores = key_scores(
            query_heads, block_data[0], block_data[2], block_data[3], own_seg, positions, causal
        )
        weights = jnp.exp(scores - log_total[..., None])
        block_len = block_data[0].shape[0]
        key_heads = block_data[0].reshape(block_len, head_count, head_size)
        value_heads = block_data[1].reshape(block_len, head_count, head_size)
        d_weights = jnp.einsum(
            "qhd,khd->hqk", grad_heads, value_heads, preferred_element_type=jnp.float32
        )
        d_scores = (weights * (d_weights - row_delta[..., None])).astype(jnp.bfloat16)
        d_query = d_query + jnp.einsum(
            "hqk,khd->qhd", d_scores, key_heads, preferred_element_type=jnp.float32
        )
        d_keys = jnp.einsum(
            "hqk,qhd->khd", d_scores, query_heads, preferred_element_type=jnp.float32
        ) * head_size ** (-0.5)
        d_values = jnp.einsum(
            "hqk,qhd->khd",
            weights.astype(jnp.bfloat16),
            grad_heads,
            preferred_element_type=jnp.float32,
        )
        return (
            d_query,
            jnp.concatenate(
                [d_keys.reshape(block_len, model_width), d_values.reshape(block_len, model_width)],
                1,
            ),
        )

    d_query, d_pairs = lax.scan(
        step_back, jnp.zeros((tok_count, head_count, head_size), jnp.float32), blocked
    )
    return (
        d_query.reshape(tok_count, model_width) * head_size ** (-0.5),
        d_pairs.reshape(keys.shape[0], 2 * model_width),
    )


def self_attend(normed, weight, head_count, own_seg, positions, seg_row):
    model_width = normed.shape[1]
    packed = plain_dot(normed, weight).astype(jnp.bfloat16)
    queries = packed[:, :model_width]
    pairs = lax.all_gather(packed[:, model_width:], "seq", axis=0, tiled=True)
    att_out, log_total = attend_forward(
        queries,
        pairs[:, :model_width],
        pairs[:, model_width:],
        head_count,
        own_seg,
        positions,
        seg_row,
        True,
        lax.axis_size("seq"),
    )
    return (att_out, log_total, queries, pairs)


def self_back(normed, weight, grad_att, kept, head_count, own_seg, positions, seg_row):
    att_out, log_total, queries, pairs = kept
    model_width = normed.shape[1]
    d_query, d_pairs = attend_back(
        queries,
        pairs[:, :model_width],
        pairs[:, model_width:],
        grad_att,
        att_out,
        log_total,
        head_count,
        own_seg,
        positions,
        seg_row,
        True,
        lax.axis_size("seq"),
    )
    d_owned = lax.psum_scatter(
        d_pairs.astype(jnp.bfloat16), "seq", scatter_dimension=0, tiled=True
    ).astype(jnp.float32)
    d_packed = jnp.concatenate([d_query, d_owned], 1).astype(jnp.bfloat16)
    return (right_dot(d_packed, weight), left_dot(normed, d_packed))


def local(
    hidden_in,
    memory,
    grad_out,
    seg_ids,
    mem_seg_ids,
    gains,
    qkv_first,
    query_cross,
    kv_cross,
    out_first,
    taps_left,
    proj_left,
    taps_right,
    proj_right,
    mid_gain,
    taps_mid,
    proj_mid,
    qkv_second,
    out_second,
    query_last,
    kv_last,
    out_last,
    ffn_up,
    ffn_down,
):
    shard_dims = (1, 0, 0, 0, 1, 1, 0, 1, 0, 0, 1, 1, 0, 0, 0, 0, 0, 0, 1)
    (
        gains,
        qkv_first,
        query_cross,
        kv_cross,
        out_first,
        taps_left,
        proj_left,
        taps_right,
        proj_right,
        mid_gain,
        taps_mid,
        proj_mid,
        qkv_second,
        out_second,
        query_last,
        kv_last,
        out_last,
        ffn_up,
        ffn_down,
    ) = (
        lax.all_gather(gains, "seq", axis=1, tiled=True),
        lax.all_gather(qkv_first, "seq", axis=0, tiled=True),
        lax.all_gather(query_cross, "seq", axis=0, tiled=True),
        lax.all_gather(kv_cross, "seq", axis=0, tiled=True),
        lax.all_gather(out_first, "seq", axis=1, tiled=True),
        lax.all_gather(taps_left, "seq", axis=1, tiled=True),
        lax.all_gather(proj_left, "seq", axis=0, tiled=True),
        lax.all_gather(taps_right, "seq", axis=1, tiled=True),
        lax.all_gather(proj_right, "seq", axis=0, tiled=True),
        lax.all_gather(mid_gain, "seq", axis=0, tiled=True),
        lax.all_gather(taps_mid, "seq", axis=1, tiled=True),
        lax.all_gather(proj_mid, "seq", axis=1, tiled=True),
        lax.all_gather(qkv_second, "seq", axis=0, tiled=True),
        lax.all_gather(out_second, "seq", axis=0, tiled=True),
        lax.all_gather(query_last, "seq", axis=0, tiled=True),
        lax.all_gather(kv_last, "seq", axis=0, tiled=True),
        lax.all_gather(out_last, "seq", axis=0, tiled=True),
        lax.all_gather(ffn_up, "seq", axis=0, tiled=True),
        lax.all_gather(ffn_down, "seq", axis=1, tiled=True),
    )
    inputs = hidden_in[0].astype(jnp.float32)
    mem_rows = memory[0]
    seg_row = seg_ids[0]
    mem_seg = mem_seg_ids[0]
    tok_count, model_width = inputs.shape
    row_start = lax.axis_index("seq") * tok_count
    positions = row_start + jnp.arange(tok_count, dtype=jnp.int32)
    own_seg = lax.dynamic_slice_in_dim(seg_row, row_start, tok_count)
    margin = jnp.full((16,), -1, jnp.int32)
    seg_padded = jnp.concatenate([margin, seg_row, margin])
    left_rim = LEFT_TAPS - 1
    right_rim = RIGHT_TAPS - 1
    seg_before = lax.dynamic_slice_in_dim(
        seg_padded, row_start + 16 - left_rim, tok_count + left_rim
    )
    seg_after = lax.dynamic_slice_in_dim(seg_padded, row_start + 16, tok_count + left_rim)
    gain_rows = gains.astype(jnp.float32)
    mid_gain_f = mid_gain.astype(jnp.float32)
    left_taps = taps_left.astype(jnp.float32)
    right_taps = taps_right.astype(jnp.float32)
    mid_taps = taps_mid.astype(jnp.float32)
    pairs_b, pairs_d = (
        lax.all_gather(
            plain_dot(mem_rows, kv_cross).astype(jnp.bfloat16), "seq", axis=0, tiled=True
        ),
        lax.all_gather(
            plain_dot(mem_rows, kv_last).astype(jnp.bfloat16), "seq", axis=0, tiled=True
        ),
    )
    normed_a = layer_norm(inputs, gain_rows[0]).astype(jnp.bfloat16)
    kept_a = self_attend(normed_a, qkv_first, H_SELF, own_seg, positions, seg_row)
    query_b = plain_dot(normed_a, query_cross).astype(jnp.bfloat16)
    out_b, total_b = attend_forward(
        query_b,
        pairs_b[:, :model_width],
        pairs_b[:, model_width:],
        H_CROSS,
        own_seg,
        positions,
        mem_seg,
        False,
        1,
    )
    joined = jnp.concatenate([kept_a[0], out_b], 1).astype(jnp.bfloat16)
    hidden_b = inputs + plain_dot(joined, out_first)
    normed_c = layer_norm(hidden_b, gain_rows[1]).astype(jnp.bfloat16)
    rim_in = passed_along(normed_c[tok_count - left_rim :], "seq", 1)
    ext_in = jnp.concatenate([rim_in, normed_c], 0).astype(jnp.float32)
    conv_l = conv_forward(ext_in, seg_before, own_seg, left_taps, left_rim).astype(jnp.bfloat16)
    conv_r = conv_forward(ext_in, seg_before, own_seg, right_taps, left_rim).astype(jnp.bfloat16)
    pre_l = plain_dot(conv_l, proj_left)
    pre_r = plain_dot(conv_r, proj_right)
    merged = jax.nn.silu(pre_l) + jnp.pad(pre_r, ((0, 0), (0, WIDE - NARROW)))
    mixed = layer_norm(merged, mid_gain_f).astype(jnp.bfloat16)
    rim_mid = passed_along(mixed[tok_count - right_rim :], "seq", 1)
    ext_mid = jnp.concatenate([rim_mid, mixed], 0).astype(jnp.float32)
    seg_mid = seg_before[left_rim - right_rim :]
    conv_m = conv_forward(ext_mid, seg_mid, own_seg, mid_taps, right_rim).astype(jnp.bfloat16)
    hidden_c = hidden_b + plain_dot(conv_m, proj_mid)
    normed_d = layer_norm(hidden_c, gain_rows[2]).astype(jnp.bfloat16)
    kept_c = self_attend(normed_d, qkv_second, H_CROSS, own_seg, positions, seg_row)
    att_c = kept_c[0].astype(jnp.bfloat16)
    hidden_d = hidden_c + plain_dot(att_c, out_second)
    normed_e = layer_norm(hidden_d, gain_rows[3]).astype(jnp.bfloat16)
    query_d = plain_dot(normed_e, query_last).astype(jnp.bfloat16)
    out_d, total_d = attend_forward(
        query_d,
        pairs_d[:, :model_width],
        pairs_d[:, model_width:],
        H_CROSS,
        own_seg,
        positions,
        mem_seg,
        False,
        1,
    )
    att_d = out_d.astype(jnp.bfloat16)
    hidden_e = hidden_d + plain_dot(att_d, out_last)
    normed_f = layer_norm(hidden_e, gain_rows[4]).astype(jnp.bfloat16)
    up_pre = plain_dot(normed_f, ffn_up)
    activ_low = jax.nn.silu(up_pre).astype(jnp.bfloat16)
    result = hidden_e + plain_dot(activ_low, ffn_down)
    grad_now = grad_out[0].astype(jnp.float32)
    branch = grad_now.astype(jnp.bfloat16)
    d_ffn_down = left_dot(activ_low, branch)
    d_up = (right_dot(branch, ffn_down) * swish_slope(up_pre)).astype(jnp.bfloat16)
    d_ffn_up = left_dot(normed_f, d_up)
    d_hidden, g_five = norm_back(hidden_e, gain_rows[4], right_dot(d_up, ffn_up))
    grad_now = grad_now + d_hidden
    branch = grad_now.astype(jnp.bfloat16)
    d_out_last = left_dot(att_d, branch)
    d_att = right_dot(branch, out_last).astype(jnp.bfloat16)
    dq_d, dkv_d_all = attend_back(
        query_d,
        pairs_d[:, :model_width],
        pairs_d[:, model_width:],
        d_att,
        out_d,
        total_d,
        H_CROSS,
        own_seg,
        positions,
        mem_seg,
        False,
        1,
    )
    dq_d = dq_d.astype(jnp.bfloat16)
    d_query_last = left_dot(normed_e, dq_d)
    d_hidden, g_four = norm_back(hidden_d, gain_rows[3], right_dot(dq_d, query_last))
    grad_now = grad_now + d_hidden
    branch = grad_now.astype(jnp.bfloat16)
    d_out_second = left_dot(att_c, branch)
    d_att = right_dot(branch, out_second).astype(jnp.bfloat16)
    d_normed, d_qkv_second = self_back(
        normed_d, qkv_second, d_att, kept_c, H_CROSS, own_seg, positions, seg_row
    )
    d_hidden, g_three = norm_back(hidden_c, gain_rows[2], d_normed)
    grad_now = grad_now + d_hidden
    branch = grad_now.astype(jnp.bfloat16)
    d_proj_mid = left_dot(conv_m, branch)
    d_conv_m = right_dot(branch, proj_mid)
    rim_back = passed_along(d_conv_m[:right_rim], "seq", -1)
    d_mixed, d_taps_mid = conv_back(
        jnp.concatenate([d_conv_m, rim_back], 0),
        seg_after[: tok_count + right_rim],
        own_seg,
        ext_mid,
        seg_mid,
        mid_taps,
        right_rim,
    )
    d_merged, d_mid_gain = norm_back(merged, mid_gain_f, d_mixed)
    d_pre_l = (d_merged * swish_slope(pre_l)).astype(jnp.bfloat16)
    d_pre_r = d_merged[:, :NARROW].astype(jnp.bfloat16)
    d_proj_left = left_dot(conv_l, d_pre_l)
    d_proj_right = left_dot(conv_r, d_pre_r)
    d_conv_l = right_dot(d_pre_l, proj_left)
    d_conv_r = right_dot(d_pre_r, proj_right)
    rim_left, rim_right = (
        passed_along(d_conv_l[:left_rim].astype(jnp.bfloat16), "seq", -1).astype(jnp.float32),
        passed_along(d_conv_r[:right_rim].astype(jnp.bfloat16), "seq", -1).astype(jnp.float32),
    )
    d_in_l, d_taps_left = conv_back(
        jnp.concatenate([d_conv_l, rim_left], 0),
        seg_after,
        own_seg,
        ext_in,
        seg_before,
        left_taps,
        left_rim,
    )
    d_in_r, d_taps_right = conv_back(
        jnp.concatenate([d_conv_r, rim_right], 0),
        seg_after[: tok_count + right_rim],
        own_seg,
        ext_in,
        seg_before,
        right_taps,
        left_rim,
    )
    d_hidden, g_two = norm_back(hidden_b, gain_rows[1], d_in_l + d_in_r)
    grad_now = grad_now + d_hidden
    branch = grad_now.astype(jnp.bfloat16)
    d_out_first = left_dot(joined, branch)
    d_joined = right_dot(branch, out_first)
    d_att_a = d_joined[:, :model_width].astype(jnp.bfloat16)
    d_att_b = d_joined[:, model_width:].astype(jnp.bfloat16)
    d_normed, d_qkv_first = self_back(
        normed_a, qkv_first, d_att_a, kept_a, H_SELF, own_seg, positions, seg_row
    )
    dq_b, dkv_b_all = attend_back(
        query_b,
        pairs_b[:, :model_width],
        pairs_b[:, model_width:],
        d_att_b,
        out_b,
        total_b,
        H_CROSS,
        own_seg,
        positions,
        mem_seg,
        False,
        1,
    )
    dq_b = dq_b.astype(jnp.bfloat16)
    d_query_cross = left_dot(normed_a, dq_b)
    d_normed = d_normed + right_dot(dq_b, query_cross)
    d_hidden, g_one = norm_back(inputs, gain_rows[0], d_normed)
    grad_in = grad_now + d_hidden
    kv_cross_f = kv_cross.astype(jnp.float32)
    kv_last_f = kv_last.astype(jnp.float32)
    dkv_b, dkv_d = (
        lax.psum_scatter(
            dkv_b_all.astype(jnp.bfloat16), "seq", scatter_dimension=0, tiled=True
        ).astype(jnp.float32),
        lax.psum_scatter(
            dkv_d_all.astype(jnp.bfloat16), "seq", scatter_dimension=0, tiled=True
        ).astype(jnp.float32),
    )
    grad_mem = jnp.einsum("me,de->md", dkv_b, kv_cross_f, precision=HIGH) + jnp.einsum(
        "me,de->md", dkv_d, kv_last_f, precision=HIGH
    )
    mem_full = mem_rows.astype(jnp.float32)
    d_kv_cross = jnp.einsum("md,me->de", mem_full, dkv_b, precision=HIGH)
    d_kv_last = jnp.einsum("md,me->de", mem_full, dkv_d, precision=HIGH)
    d_gains = jnp.stack([g_one, g_two, g_three, g_four, g_five], 0)
    seq_count = lax.axis_size("seq")
    row_count = lax.axis_size("rows")
    listed = (
        d_gains,
        d_qkv_first,
        d_query_cross,
        d_kv_cross,
        d_out_first,
        d_taps_left,
        d_proj_left,
        d_taps_right,
        d_proj_right,
        d_mid_gain,
        d_taps_mid,
        d_proj_mid,
        d_qkv_second,
        d_out_second,
        d_query_last,
        d_kv_last,
        d_out_last,
        d_ffn_up,
        d_ffn_down,
    )
    blocks = [
        jnp.moveaxis(piece, axis_dim, 0).reshape(seq_count, -1)
        for piece, axis_dim in zip(listed, shard_dims)
    ]
    widths = [block.shape[1] for block in blocks]
    stacked = jnp.concatenate(blocks, 1)
    total_len = stacked.shape[1]
    padded_len = -(-total_len // row_count) * row_count
    ordered = jnp.swapaxes(
        stacked.reshape(seq_count, row_count, padded_len // row_count), 0, 1
    ).reshape(-1)
    piece_sum = lax.psum_scatter(ordered, ("rows", "seq"), scatter_dimension=0, tiled=True)
    own_share = lax.all_gather(piece_sum.astype(jnp.bfloat16), "rows", axis=0, tiled=True).astype(
        piece_sum.dtype
    )
    shares = []
    offset = 0
    for piece, axis_dim, width in zip(listed, shard_dims, widths):
        moved_shape = jnp.moveaxis(piece, axis_dim, 0).shape
        local_shape = (moved_shape[0] // seq_count,) + tuple(moved_shape[1:])
        shares.append(
            jnp.moveaxis(own_share[offset : offset + width].reshape(local_shape), 0, axis_dim)
        )
        offset = offset + width
    return (
        result.astype(jnp.bfloat16)[None],
        grad_in[None],
        grad_mem[None],
        shares[0],
        shares[1],
        shares[2],
        shares[3],
        shares[4],
        shares[5],
        shares[6],
        shares[7],
        shares[8],
        shares[9],
        shares[10],
        shares[11],
        shares[12],
        shares[13],
        shares[14],
        shares[15],
        shares[16],
        shares[17],
        shares[18],
    )


def solution(mesh):
    placed = (
        P("rows", "seq", None),
        P("rows", "seq", None),
        P("rows", "seq", None),
        P("rows", None),
        P("rows", None),
        P(None, "seq"),
        P("seq", None),
        P("seq", None),
        P("seq", None),
        P(None, "seq"),
        P(None, "seq"),
        P("seq", None),
        P(None, "seq"),
        P("seq", None),
        P("seq"),
        P(None, "seq"),
        P(None, "seq"),
        P("seq", None),
        P("seq", None),
        P("seq", None),
        P("seq", None),
        P("seq", None),
        P("seq", None),
        P(None, "seq"),
    )
    return jax.shard_map(
        local,
        mesh=mesh,
        in_specs=placed,
        out_specs=(
            P("rows", "seq", None),
            P("rows", "seq", None),
            P("rows", "seq", None),
            P(None, "seq"),
            P("seq", None),
            P("seq", None),
            P("seq", None),
            P(None, "seq"),
            P(None, "seq"),
            P("seq", None),
            P(None, "seq"),
            P("seq", None),
            P("seq"),
            P(None, "seq"),
            P(None, "seq"),
            P("seq", None),
            P("seq", None),
            P("seq", None),
            P("seq", None),
            P("seq", None),
            P("seq", None),
            P(None, "seq"),
        ),
        check_vma=False,
    )
```

profile of v0, /device:TPU:0, one launch (start us, length us, event | category | flops | bytes accessed | tf_op | source)
XLA Modules:
  0.0 2050.5 jit_solution(18270075293391895963)
XLA Ops:
  15.2 24.4 %all-gather.13.cloned.1.call-done = bf16[512,1536]{1,0:T(8,128)(2,1)} async-done(((bf16[256,1536]{1,0:T(8,128)(2,1)}), bf16[512,1536]{1,0:T(8,128)(2,1)}) %all-gather.13.cloned.1.call-update) | async-done | bytes 1572880 | tf_op jit(solution)/shard_map/all_gather | solution.py:314
  89.6 16.8 all-gather.15.cloned.1.call-done
  111.7 46.8 %while.19 = (s32[]{:T(128)}, f32[16,640]{1,0:T(8,128)S(1)}, f32[16,640]{1,0:T(8,128)S(1)}, s32[2,640]{1,0:T(2,128)S(1)}, s32[640]{0:T(1024)S(1)}, /*index=5*/s32...) while((s32[]{:T(128)}, f32[16,640]{1,0:T(8,128)S(1)}, ...), condition=%wide.region_5.6_spmd.clone, body=%wide.region_2.5_spmd.clone.sunk | while | flops 466586240 | bytes 56834696 | solution.py:133
  123.4 11.7 exponential_reduce_fusion.6
  146.7 11.7 exponential_reduce_fusion.6
  158.5 27.8 %while.20 = (s32[]{:T(128)}, f32[640,16,32]{0,2,1:T(8,128)}, bf16[2,640,512]{1,2,0:T(8,128)(2,1)S(1)}, s32[2,640]{1,0:T(2,128)S(1)}, s32[640]{0:T(1024)S(1)}, /*...) while((s32[]{:T(128)}, f32[640,16,32]{0,2,1:T(8,128)}, ...), condition=%wide.region_7.8_spmd.clone, body=%wide.region_6.7_spmd.clone.sunk | while | flops 866960000 | bytes 8092307 | solution.py:150
  254.5 15.2 all_gather.91
  269.7 14.9 all_gather.92
  286.2 12.7 all_gather.90
  306.0 13.2 while.21
  319.2 16.2 while.22
  353.3 15.7 all-gather.33.cloned.1.call-done
  391.6 62.4 %while.23 = (s32[]{:T(128)}, f32[640,8,64]{0,2,1:T(8,128)}, bf16[2,640,1024]{2,1,0:T(8,128)(2,1)}, bf16[2,640,512]{1,2,0:T(8,128)(2,1)}, s32[2,640]{1,0:T(2,128)...) while((s32[]{:T(128)}, f32[640,8,64]{0,2,1:T(8,128)}, ...), condition=%wide.region_35.36_spmd.clone, body=%wide.region_34.35_spmd.clone.sunk | while | flops 2135081600 | bytes 84544232 | solution.py:213
  464.9 27.0 %reduce-scatter.9.cloned.1.call-done = bf16[640,1024]{1,0:T(8,128)(2,1)} async-done(((bf16[1280,1024]{1,0:T(8,128)(2,1)}), bf16[640,1024]{1,0:T(8,128)(2,1)}) %reduce-scatter.9.cloned.1.call-update) | async-done | bytes 1310736 | tf_op jit(solution)/shard_map/reduce_scatter | solution.py:258
  530.3 19.2 multiply_reduce_fusion.32
  571.5 121.3 %while.24 = (s32[]{:T(128)}, f32[640,16,32]{0,2,1:T(8,128)S(1)}, bf16[2,640,1024]{2,1,0:T(8,128)(2,1)}, bf16[2,640,512]{1,2,0:T(8,128)(2,1)}, s32[2,640]{1,0:T(2...) while((s32[]{:T(128)}, f32[640,16,32]{0,2,1:T(8,128)S(1)}, ...), condition=%wide.region_45.46_spmd.clone, body=%wide.region_44.45_spmd.clone.sunk | while | flops 2167849472 | bytes 153090864 | solution.py:213
  596.7 16.0 fusion.436
  657.0 16.0 fusion.436
  845.4 65.3 %reshape.1122 = f32[7491072]{0:T(1024)} reshape(f32[2,3745536]{1,0:T(2,128)} %constant_dynamic-update-slice_fusion.2) | data formatting | bytes 59928576
  910.6 37.7 %reshape.1055 = f32[2,16,234096]{2,1,0:T(8,128)} reshape(f32[7491072]{0:T(1024)} %reshape.1122) | data formatting | bytes 59928576 | tf_op jit(solution)/shard_map/reshape | solution.py:571
  948.3 50.0 %copy.393 = f32[2,16,234096]{2,0,1:T(2,128)} copy(f32[2,16,234096]{2,1,0:T(8,128)} %reshape.1055) | data formatting | bytes 59928576 | tf_op jit(solution)/shard_map/reshape | solution.py:571
  998.3 354.4 %while.25 = (u32[]{:T(128)}, f32[16,2,234096]{2,1,0:T(2,128)}, f32[7491072]{0:T(1024)}, u32[]{}, u32[]{}, /*index=5*/u32[]{}, u32[]{}) while((u32[]{:T(128)}, f32[16,2,234096]{2,1,0:T(2,128)}, f32[7491072]{0:T(1024)}, u32[]{}, u32[]{}, /*index=5*/u32[]{}, u32[]{}) %tuple.381), condition=%wide.cond, body=%wide.body.sunk | while | flops 9 | bytes 22473396
  1009.8 32.7 %dynamic-update-slice.41 = f32[7491072]{0:T(1024)} dynamic-update-slice(f32[7491072]{0:T(1024)} %get-tuple-element.2095, f32[936384]{0:T(1024)} %reshape.1126, u32[]{:T(128)S(6)} %add.848) | dynamic-update-slice | bytes 7491076
  1054.0 32.8 %dynamic-update-slice.41 = f32[7491072]{0:T(1024)} dynamic-update-slice(f32[7491072]{0:T(1024)} %get-tuple-element.2095, f32[936384]{0:T(1024)} %reshape.1126, u32[]{:T(128)S(6)} %add.848) | dynamic-update-slice | bytes 7491076
  1098.4 32.9 %dynamic-update-slice.41 = f32[7491072]{0:T(1024)} dynamic-update-slice(f32[7491072]{0:T(1024)} %get-tuple-element.2095, f32[936384]{0:T(1024)} %reshape.1126, u32[]{:T(128)S(6)} %add.848) | dynamic-update-slice | bytes 7491076
  1142.8 32.7 %dynamic-update-slice.41 = f32[7491072]{0:T(1024)} dynamic-update-slice(f32[7491072]{0:T(1024)} %get-tuple-element.2095, f32[936384]{0:T(1024)} %reshape.1126, u32[]{:T(128)S(6)} %add.848) | dynamic-update-slice | bytes 7491076
  1187.0 32.8 %dynamic-update-slice.41 = f32[7491072]{0:T(1024)} dynamic-update-slice(f32[7491072]{0:T(1024)} %get-tuple-element.2095, f32[936384]{0:T(1024)} %reshape.1126, u32[]{:T(128)S(6)} %add.848) | dynamic-update-slice | bytes 7491076
  1231.3 32.8 %dynamic-update-slice.41 = f32[7491072]{0:T(1024)} dynamic-update-slice(f32[7491072]{0:T(1024)} %get-tuple-element.2095, f32[936384]{0:T(1024)} %reshape.1126, u32[]{:T(128)S(6)} %add.848) | dynamic-update-slice | bytes 7491076
  1275.7 32.8 %dynamic-update-slice.41 = f32[7491072]{0:T(1024)} dynamic-update-slice(f32[7491072]{0:T(1024)} %get-tuple-element.2095, f32[936384]{0:T(1024)} %reshape.1126, u32[]{:T(128)S(6)} %add.848) | dynamic-update-slice | bytes 7491076
  1320.0 32.7 %dynamic-update-slice.41 = f32[7491072]{0:T(1024)} dynamic-update-slice(f32[7491072]{0:T(1024)} %get-tuple-element.2095, f32[936384]{0:T(1024)} %reshape.1126, u32[]{:T(128)S(6)} %add.848) | dynamic-update-slice | bytes 7491076
  1352.7 481.8 %all-reduce.7 = bf16[7491072]{0:T(1024)(128)(2,1)} all-reduce(f32[7491072]{0:T(1024)} %get-tuple-element.1078), channel_id=6, replica_groups=mesh['rows'=16,'seq'=2] {'rows','seq'}, use_global_device_ids=true, to_apply=%region_83.84.clone | all-reduce | flops 7491072 | bytes 44946432
  1858.7 145.1 %all-reduce.6.cloned.1.call-done = bf16[3745536]{0:T(1024)(128)(2,1)} async-done(((bf16[3745536]{0:T(1024)(128)(2,1)}), bf16[3745536]{0:T(1024)(128)(2,1)}) %all-reduce.6.cloned.1.call-update) | async-done | bytes 7491088
  (1049 shorter events, 786.9 us)
Async XLA Ops:
  7.2 61.7 %copy-start = (bf16[1,128,512]{2,1,0:T(8,128)(2,1)S(1)}, bf16[1,128,512]{2,1,0:T(8,128)(2,1)}, u32[]{:S(2)}) copy-start(bf16[1,128,512]{2,1,0:T(8,128)(2,1)} %param.37) | copy-start | bytes 393220
  7.2 32.3 %all-gather.13.cloned.1.call-start = ((), (), s32[]{:S(2)}) async-start(), calls=%async_computation.4 | async-start | bytes 2359296 | tf_op jit(solution)/shard_map/all_gather | solution.py:314
  8.0 60.9 %all-gather.17.cloned.1.call-start = ((), (), s32[]{:S(2)}) async-start(), calls=%async_computation.6 | async-start | bytes 1572864 | tf_op jit(solution)/shard_map/all_gather | solution.py:316
  8.7 97.6 %all-gather.15.cloned.1.call-start = ((), (), s32[]{:S(2)}) async-start(), calls=%async_computation.5 | async-start | bytes 3932160 | tf_op jit(solution)/shard_map/all_gather | solution.py:226
  9.0 59.1 %copy-start.143 = (f32[640]{0:T(1024)}, f32[640]{0:T(1024)S(1)}, u32[]{:S(2)}) copy-start(f32[640]{0:T(1024)S(1)} %broadcast_multiply_fusion.17) | copy-start | bytes 7684
  14.6 53.5 %copy-start.150 = (f32[640]{0:T(1024)}, f32[640]{0:T(1024)S(1)}, u32[]{:S(2)}) copy-start(f32[640]{0:T(1024)S(1)} %add_rsqrt_fusion.5) | copy-start | bytes 7684
  15.2 52.9 %copy-start.163 = (f32[1,512]{1,0:T(1,128)}, f32[1,512]{1,0:T(1,128)S(1)}, u32[]{:S(2)}) copy-start(f32[1,512]{1,0:T(1,128)S(1)} %get-tuple-element.1351) | copy-start | bytes 6148
  44.8 144.8 %all-gather.19.cloned.1.call-start = ((), (), s32[]{:S(2)}) async-start(), calls=%async_computation.7 | async-start | bytes 1572864 | tf_op jit(solution)/shard_map/all_gather | solution.py:317
  45.4 176.1 %all-gather.21.cloned.1.call-start = ((), (), s32[]{:S(2)}) async-start(), calls=%async_computation.8 | async-start | bytes 1572864 | tf_op jit(solution)/shard_map/all_gather | solution.py:319
  46.0 191.3 %all-gather.23.cloned.1.call-start = ((), (), s32[]{:S(2)}) async-start(), calls=%async_computation.9 | async-start | bytes 1572864 | tf_op jit(solution)/shard_map/all_gather | solution.py:324
  46.6 193.7 %all-gather.25.cloned.1.call-start = ((), (), s32[]{:S(2)}) async-start(), calls=%async_computation.10 | async-start | bytes 2359296 | tf_op jit(solution)/shard_map/all_gather | solution.py:325
  47.3 237.3 %all-gather.29.cloned.1.call-start = ((), (), s32[]{:S(2)}) async-start(), calls=%async_computation.12 | async-start | bytes 1572864 | tf_op jit(solution)/shard_map/all_gather | solution.py:328
  48.1 252.9 %all-gather.27.cloned.1.call-start = ((), (), s32[]{:S(2)}) async-start(), calls=%async_computation.11 | async-start | bytes 3932160 | tf_op jit(solution)/shard_map/all_gather | solution.py:226
  193.6 20.6 %collective-permute-start = (bf16[10,512]{1,0:T(8,128)(2,1)S(1)}, bf16[10,512]{1,0:T(8,128)(2,1)S(1)}, u32[]{:S(2)}, u32[]{:S(2)}) collective-permute-start(bf16[10,512]{1,0:T(8,128)(2,1)S(1)} %slice.688), channel_id=1, source_target_pairs={{0,1},{2,3},{4,5},{6,7},{8,9},{10,11},{12,13},{14,15},{16,17},{18,... | collective-permute-start | bytes 30728 | tf_op jit(solution)/shard_map/ppermute | solution.py:22
  227.6 3.5 collective-permute-start.1
  244.5 102.8 %all-gather.31.cloned.1.call-start = ((), (), s32[]{:S(2)}) async-start(), calls=%async_computation.13 | async-start | bytes 3145728 | tf_op jit(solution)/shard_map/all_gather | solution.py:330
  245.1 123.9 %all-gather.33.cloned.1.call-start = ((), (), s32[]{:S(2)}) async-start(), calls=%async_computation.14 | async-start | bytes 3145728 | tf_op jit(solution)/shard_map/all_gather | solution.py:331
  245.9 245.9 %reduce-scatter.9.cloned.1.call-start = ((), (), s32[]{:S(2)}) async-start(), calls=%async_computation.15 | async-start | bytes 3932160 | tf_op jit(solution)/shard_map/reduce_scatter | solution.py:258
  454.1 281.4 %reduce-scatter.15.cloned.1.call-start = ((), (), s32[]{:S(2)}) async-start(), calls=%async_computation.19 | async-start | bytes 786432
  456.6 51.5 %copy-start.249 = (pred[640]{0:T(1024)(128)(4,1)}, pred[640]{0:T(1024)(128)(4,1)S(1)}, u32[]{:S(2)}) copy-start(pred[640]{0:T(1024)(128)(4,1)S(1)} %get-tuple-element.1338) | copy-start | bytes 1924
  456.6 51.5 %copy-start.250 = (pred[640]{0:T(1024)(128)(4,1)}, pred[640]{0:T(1024)(128)(4,1)S(1)}, u32[]{:S(2)}) copy-start(pred[640]{0:T(1024)(128)(4,1)S(1)} %get-tuple-element.1339) | copy-start | bytes 1924
  456.6 51.5 %copy-start.251 = (pred[640]{0:T(1024)(128)(4,1)}, pred[640]{0:T(1024)(128)(4,1)S(1)}, u32[]{:S(2)}) copy-start(pred[640]{0:T(1024)(128)(4,1)S(1)} %get-tuple-element.1340) | copy-start | bytes 1924
  456.6 51.5 %copy-start.252 = (pred[640]{0:T(1024)(128)(4,1)}, pred[640]{0:T(1024)(128)(4,1)S(1)}, u32[]{:S(2)}) copy-start(pred[640]{0:T(1024)(128)(4,1)S(1)} %get-tuple-element.1341) | copy-start | bytes 1924
  456.6 51.5 %copy-start.253 = (pred[640]{0:T(1024)(128)(4,1)}, pred[640]{0:T(1024)(128)(4,1)S(1)}, u32[]{:S(2)}) copy-start(pred[640]{0:T(1024)(128)(4,1)S(1)} %get-tuple-element.1342) | copy-start | bytes 1924
  456.6 51.5 %copy-start.254 = (pred[640]{0:T(1024)(128)(4,1)}, pred[640]{0:T(1024)(128)(4,1)S(1)}, u32[]{:S(2)}) copy-start(pred[640]{0:T(1024)(128)(4,1)S(1)} %get-tuple-element.1343) | copy-start | bytes 1924
  456.7 51.5 %copy-start.255 = (pred[640]{0:T(1024)(128)(4,1)}, pred[640]{0:T(1024)(128)(4,1)S(1)}, u32[]{:S(2)}) copy-start(pred[640]{0:T(1024)(128)(4,1)S(1)} %get-tuple-element.1344) | copy-start | bytes 1924
  502.2 5.9 collective-permute-start.2
  519.1 7.2 collective-permute-start.4
  523.6 5.7 collective-permute-start.3
  526.2 264.7 %reduce-scatter.13.cloned.1.call-start = ((), (), s32[]{:S(2)}) async-start(), calls=%async_computation.18 | async-start | bytes 786432
  569.6 229.5 %reduce-scatter.11.cloned.1.call-start = ((), (), s32[]{:S(2)}) async-start(), calls=%async_computation.16 | async-start | bytes 3932160 | tf_op jit(solution)/shard_map/reduce_scatter | solution.py:258
  693.8 1310.0 %all-reduce.6.cloned.1.call-start = ((), (), s32[]{:S(2)}) async-start(), calls=%async_computation.17 | async-start | bytes 14983168
  (293 other events, 1774.6 us)
Sparse Core Ops, SparseCore 0:
  9.6 29.8 all-gather.12
  41.1 22.1 all-gather.16
  65.4 40.8 all-gather.14
  107.7 21.2 all-gather.18
  130.4 21.2 all-gather.20
  153.2 21.2 all-gather.22
  176.0 30.0 all-gather.24
  207.6 21.6 all-gather.28
  244.6 54.9 all-gather.26
  301.0 33.2 all-gather.30
  335.9 33.0 all-gather.32
  454.2 37.5 reduce-scatter.8
  526.3 17.1 reduce-scatter.14
  569.7 14.5 reduce-scatter.12
  692.9 37.5 reduce-scatter.10
  1847.5 156.2 all-reduce.5
where the time goes:
time: 2080 us; the launch traced here: 2050 us
  local copies, waits for them, and re-layouts  743 us (36%)
  blocking collectives  584 us (28%)
  matrix products  350 us (17%)
  waiting for transfers between devices  243 us (12%)
  other arithmetic  100 us (5%)
    unnamed x645, local copies, waits for them, and re-layouts  503 us
    unnamed x1, blocking collectives  482 us
    unnamed x19, waiting for transfers between devices  151 us
    reshape x2, local copies, waits for them, and re-layouts, local(): stacked.reshape(seq_count, row_count, padded_len // row_count)  87.7 us
    dot_general x10, matrix products, key_scores(): jnp.einsum('qhd,khd->hqk', query_heads, key_heads, preferred_element_type...  63 us
    reshape x19, local copies, waits for them, and re-layouts, local(): jnp.moveaxis(piece, axis_dim, 0).reshape(seq_count, -1)  56.3 us
    dot_general x6, matrix products, step_back(): jnp.einsum('qhd,khd->hqk', grad_heads, value_heads, preferred_element_typ...  55.8 us
    dot_general x6, matrix products, step_back(): jnp.einsum('hqk,qhd->khd', weights.astype(jnp.bfloat16), grad_heads, pref...  46.5 us
  transfers between devices with their start and end apart: 21, of which 8 were waited for; matrix products, arithmetic and copies ran while one was open for 23% of the time, Pallas kernels for 0%

commit v1 on v0

v1 whole, which is shorter than its diff:
```python
import functools

import jax
import jax.numpy as jnp
from jax import lax
from jax.experimental import pallas as pl
from jax.experimental.pallas import tpu as pltpu
from jax.sharding import PartitionSpec as P

H_SELF = 16
H_CROSS = 8
WIDE = 1024
NARROW = 256
LEFT_TAPS = 11
RIGHT_TAPS = 7


NEG_BIG = -1e30
EPSILON = 1e-06


def rotated(block, axis, distance):
    size = lax.axis_size(axis)
    return lax.ppermute(block, axis, [((i + distance) % size, i) for i in range(size)])


def core_swapped(block):
    return lax.ppermute(block, "rows", [(i, i ^ 1) for i in range(lax.axis_size("rows"))])


def in_place_order(relative, dim):
    count = len(relative)
    place = lax.axis_index("seq")
    orders = [
        jnp.concatenate([relative[(p - me) % count] for p in range(count)], dim)
        for me in range(count)
    ]
    result = orders[0]
    for me in range(1, count):
        result = jnp.where(place == me, orders[me], result)
    return result


def gathered(block, dim=0):
    count = lax.axis_size("seq")
    return in_place_order([block] + [rotated(block, "seq", d) for d in range(1, count)], dim)


def core_half(shard):
    half = shard.shape[0] // 2
    return lax.dynamic_slice_in_dim(shard, (lax.axis_index("rows") & 1) * half, half)


def flat_half(shard, dim):
    part = core_half(shard)
    if dim == 0:
        return part
    width = shard.shape[1]
    blocks = part.reshape(-1, width // 2, width)
    return jnp.swapaxes(blocks, 0, 1).reshape(width // 2, -1)


def unflat_half(part, shape, dim):
    if dim == 0:
        return part
    width = shape[1]
    blocks = part.reshape(width // 2, -1, width)
    return jnp.swapaxes(blocks, 0, 1).reshape(shape[0] // 2, width)


def group_gather(shards, dims, earlier):
    packed = jnp.concatenate([flat_half(shard, dim) for shard, dim in zip(shards, dims)], 1)
    packed, _ = after(packed, earlier)
    core = lax.axis_index("rows") & 1
    pieces = []
    for d in range(1, lax.axis_size("seq")):
        same = rotated(packed, "seq", d)
        pieces.append((same, core_swapped(same)))
    results = []
    offset = 0
    for shard, dim in zip(shards, dims):
        size = shard.size // 2 // packed.shape[0]
        relative = [shard]
        for same, other in pieces:
            same = unflat_half(same[:, offset : offset + size], shard.shape, dim)
            other = unflat_half(other[:, offset : offset + size], shard.shape, dim)
            relative.append(
                jnp.where(core == 0, jnp.concatenate([same, other], 0), jnp.concatenate([other, same], 0))
            )
        results.append(in_place_order(relative, dim))
        offset = offset + size
    return results, pieces[-1][0]


def small_gather(shards, dims, earlier):
    sizes = [shard.size for shard in shards]
    flat = jnp.concatenate([shard.reshape(-1) for shard in shards])
    flat, _ = after(padded_rows(flat, 2048, 0).reshape(-1, 128), earlier)
    parts = [flat] + [rotated(flat, "seq", d) for d in range(1, lax.axis_size("seq"))]
    parts = [part.reshape(-1) for part in parts]
    results = []
    offset = 0
    for shard, dim, size in zip(shards, dims, sizes):
        relative = [part[offset : offset + size].reshape(shard.shape) for part in parts]
        results.append(in_place_order(relative, dim))
        offset = offset + size
    return results, parts[-1]


def padded_rows(block, multiple, dim):
    extra = -block.shape[dim] % multiple
    if not extra:
        return block
    widths = [(0, 0)] * block.ndim
    widths[dim] = (0, extra)
    return jnp.pad(block, widths)


def small_columns(grads, width):
    seq_count = lax.axis_size("seq")
    rows = [
        jnp.moveaxis(grad.reshape(-1, seq_count, grad.shape[-1] // (seq_count * width), width), 1, 2).reshape(
            -1, seq_count * width
        )
        for grad in grads
    ]
    return padded_rows(jnp.concatenate(rows, 0), 128, 0).T.astype(jnp.bfloat16)


def small_shares(columns, grads, width):
    seq_count = lax.axis_size("seq")
    rows = columns.T
    results = []
    offset = 0
    for grad in grads:
        count = grad.size // (seq_count * width)
        shape = grad.shape[:-1] + (grad.shape[-1] // seq_count,)
        results.append(rows[offset : offset + count].reshape(shape))
        offset = offset + count
    return results


def halved_sum(block, axis, bit, dim):
    half = block.shape[dim] // 2
    upper = ((lax.axis_index(axis) & bit) != 0).astype(jnp.int32)
    kept = lax.dynamic_slice_in_dim(block, upper * half, half, dim)
    sent = lax.dynamic_slice_in_dim(block, (1 - upper) * half, half, dim)
    got = lax.ppermute(sent, axis, [(i, i ^ bit) for i in range(lax.axis_size(axis))])
    return (kept.astype(jnp.float32) + got.astype(jnp.float32)).astype(jnp.bfloat16)


def row_sum_owned(partial):
    bit = lax.axis_size("seq") // 2
    while bit:
        partial = halved_sum(partial, "seq", bit, 0)
        bit = bit // 2
    return partial.astype(jnp.float32)


def after(values, others):
    return lax.optimization_barrier((values, others))


def offload_rows(packed):
    seq_count = lax.axis_size("seq")
    row_count = lax.axis_size("rows")
    blocks = packed.reshape(seq_count, row_count, -1, packed.shape[1])
    blocks = jnp.swapaxes(blocks, 0, 1).reshape(packed.shape)
    return lax.psum_scatter(blocks, "rows", scatter_dimension=0, tiled=True)


def offload_seq(blocks):
    return lax.psum_scatter(blocks, "seq", scatter_dimension=0, tiled=True)


def offload_back(share):
    return lax.all_gather(share, "rows", axis=0, tiled=True)


def passed_along(block, axis, distance):
    devices = range(lax.axis_size(axis))
    route = [(i - distance, i) for i in devices if i - distance in devices]
    return lax.ppermute(block, axis, route)


def layer_norm(values, gain_vec):
    centre = values - jnp.mean(values, axis=-1, keepdims=True)
    inverse = lax.rsqrt(jnp.mean(centre * centre, axis=-1, keepdims=True) + EPSILON)
    return centre * inverse * gain_vec


def norm_back(values, gain_vec, upstream):
    centre = values - jnp.mean(values, axis=-1, keepdims=True)
    inverse = lax.rsqrt(jnp.mean(centre * centre, axis=-1, keepdims=True) + EPSILON)
    normed = centre * inverse
    scaled = upstream * gain_vec
    d_values = inverse * (
        scaled
        - jnp.mean(scaled, axis=-1, keepdims=True)
        - normed * jnp.mean(scaled * normed, axis=-1, keepdims=True)
    )
    return (d_values, jnp.sum(upstream * normed, axis=0))


def swish_slope(pre_act):
    sigma = jax.nn.sigmoid(pre_act)
    return sigma * (1.0 + pre_act * (1.0 - sigma))


def plain_dot(first, second):
    return jnp.dot(first, second, preferred_element_type=jnp.float32)


def left_dot(first, second):
    return jnp.einsum("nk,nm->km", first, second, preferred_element_type=jnp.float32)


def right_dot(grads_in, weight):
    return jnp.einsum("nm,km->nk", grads_in, weight, preferred_element_type=jnp.float32)


TILE = 256
SEG_ROWS = 16
LOG2E = 1.4426950408889634


def tiles_of(extent):
    return [(low, min(low + TILE, extent)) for low in range(0, extent, TILE)]


def tn_dot(first, second):
    return lax.dot_general(first, second, (((0,), (0,)), ((), ())), preferred_element_type=jnp.float32)


def nn_dot(first, second):
    return lax.dot_general(first, second, (((1,), (0,)), ((), ())), preferred_element_type=jnp.float32)


def nt_dot(first, second):
    return lax.dot_general(first, second, (((1,), (1,)), ((), ())), preferred_element_type=jnp.float32)


def row_numbers(width):
    return lax.broadcasted_iota(jnp.int32, (SEG_ROWS, width), 0)


def split_low(values, count):
    pieces = []
    for _ in range(count):
        piece = values.astype(jnp.bfloat16).astype(jnp.float32)
        pieces.append(piece)
        values = values - piece
    return pieces


def key_marks(key_seg, ones):
    rows = row_numbers(key_seg.shape[1])
    marked = jnp.logical_or(rows == key_seg, jnp.logical_and(rows >= 3, rows < 3 + ones))
    return jnp.where(marked, 1.0, 0.0).astype(jnp.bfloat16)


def query_marks(query_seg):
    rows = row_numbers(query_seg.shape[1])
    other = jnp.logical_and(rows < 3, rows != query_seg)
    return jnp.where(other, NEG_BIG, 0.0)


def with_rows(marks, first, pieces):
    rows = row_numbers(marks.shape[1])
    for k, piece in enumerate(pieces):
        marks = jnp.where(rows == first + k, piece, marks)
    return marks.astype(jnp.bfloat16)


def triangle(scores, low):
    key_at = lax.broadcasted_iota(jnp.int32, scores.shape, 0)
    query_at = lax.broadcasted_iota(jnp.int32, scores.shape, 1) + low
    return jnp.where(key_at <= query_at, scores, NEG_BIG)


def masked_scores(key_block, query_block, low, causal):
    scores = tn_dot(key_block, query_block)
    if not causal:
        return scores
    if low == 0:
        return triangle(scores, 0)
    return jnp.concatenate([scores[:low], triangle(scores[low:], 0)], 0)


def attend_kernel(heads, causal, place_ref, qt_ref, pair_ref, qseg_ref, kseg_ref, ot_ref, total_ref, kmark_ref):
    width, tokens = qt_ref.shape
    size = width // heads
    factor = size ** (-0.5) * LOG2E
    block = tokens if causal else pair_ref.shape[1]
    place = place_ref[0] if causal else 0
    kmark_ref[...] = key_marks(kseg_ref[...], 0)
    value_marks = jnp.where(row_numbers(block) == 0, 1.0, 0.0).astype(jnp.bfloat16)
    qmarks = query_marks(qseg_ref[...]).astype(jnp.bfloat16)

    def one_head(head, carry):
        own = pl.ds(pl.multiple_of(head * size, size), size)
        also = pl.ds(pl.multiple_of(width + head * size, size), size)
        query_rows = jnp.concatenate([qt_ref[own, :], qmarks], 0)

        def keys_at(start, count):
            lanes = pl.ds(pl.multiple_of(start, 128), count)
            return (
                jnp.concatenate([pair_ref[own, lanes], kmark_ref[:, lanes]], 0),
                jnp.concatenate([pair_ref[also, lanes], value_marks[:, :count]], 0),
            )

        for low, high in tiles_of(tokens):
            query_tile = query_rows[:, low:high]
            count = high if causal else block
            key_rows, value_rows = keys_at(place * block, count)
            scores = masked_scores(key_rows, query_tile, low, causal)
            peak = jnp.max(scores, axis=0, keepdims=True)
            weights = jnp.exp2((scores - peak) * factor).astype(jnp.bfloat16)
            summed = nn_dot(value_rows, weights)
            if causal:

                def earlier(step, state):
                    peak, summed = state
                    key_rows, value_rows = keys_at(step * block, block)
                    scores = tn_dot(key_rows, query_tile)
                    new_peak = jnp.maximum(peak, jnp.max(scores, axis=0, keepdims=True))
                    weights = jnp.exp2((scores - new_peak) * factor).astype(jnp.bfloat16)
                    summed = summed * jnp.exp2((peak - new_peak) * factor) + nn_dot(value_rows, weights)
                    return (new_peak, summed)

                peak, summed = lax.fori_loop(0, place, earlier, (peak, summed))
            total = summed[size : size + 1]
            ot_ref[own, low:high] = (summed[:size] / total).astype(jnp.bfloat16)
            total_ref[head, :, low:high] = peak + jnp.log2(total) / factor
        return carry

    lax.fori_loop(0, heads, one_head, 0)


def attend_back_kernel(
    heads, causal, place_ref, qt_ref, pair_ref, gt_ref, ot_ref, total_ref, qseg_ref, kseg_ref,
    dq_ref, dpair_ref, kmark_ref, dkh_ref, dvh_ref,
):
    width, tokens = qt_ref.shape
    size = width // heads
    scale = size ** (-0.5)
    factor = scale * LOG2E
    block = tokens if causal else pair_ref.shape[1]
    place = place_ref[0] if causal else 0
    kmark_ref[...] = key_marks(kseg_ref[...], 3)
    value_marks = jnp.where(row_numbers(block) < 2, 1.0, 0.0).astype(jnp.bfloat16)
    qmarks = query_marks(qseg_ref[...])

    def one_head(head, carry):
        own = pl.ds(pl.multiple_of(head * size, size), size)
        also = pl.ds(pl.multiple_of(width + head * size, size), size)
        query_plain = qt_ref[own, :]
        grad_plain = gt_ref[own, :]
        delta = jnp.sum(
            grad_plain.astype(jnp.float32) * ot_ref[own, :].astype(jnp.float32), axis=0, keepdims=True
        )
        total = total_ref[head]
        query_rows = jnp.concatenate([query_plain, with_rows(qmarks, 3, split_low(-total, 3))], 0)
        grad_rows = jnp.concatenate(
            [grad_plain, with_rows(jnp.zeros_like(qmarks), 0, split_low(-delta, 2))], 0
        )
        dkh_ref[...] = jnp.zeros_like(dkh_ref)
        dvh_ref[...] = jnp.zeros_like(dvh_ref)

        def on_block(start, count, low, high, diagonal):
            lanes = pl.ds(pl.multiple_of(start, 128), count)
            key_plain = pair_ref[own, lanes]
            key_rows = jnp.concatenate([key_plain, kmark_ref[:, lanes]], 0)
            value_rows = jnp.concatenate([pair_ref[also, lanes], value_marks[:, :count]], 0)
            scores = masked_scores(key_rows, query_rows[:, low:high], low, diagonal)
            weights = jnp.exp2(scores * factor)
            slopes = tn_dot(value_rows, grad_rows[:, low:high])
            d_scores = (weights * slopes).astype(jnp.bfloat16)
            dvh_ref[:, lanes] += nt_dot(grad_plain[:, low:high], weights.astype(jnp.bfloat16))
            dkh_ref[:, lanes] += nt_dot(query_plain[:, low:high], d_scores)
            return nn_dot(key_plain, d_scores)

        for low, high in tiles_of(tokens):
            d_query = on_block(place * block, high if causal else block, low, high, causal)
            if causal:
                d_query = lax.fori_loop(
                    0,
                    place,
                    lambda step, held: held + on_block(step * block, block, low, high, False),
                    d_query,
                )
            dq_ref[own, low:high] = (d_query * scale).astype(jnp.bfloat16)
        dpair_ref[own, :] = (dkh_ref[...] * scale).astype(jnp.bfloat16)
        dpair_ref[also, :] = dvh_ref[...].astype(jnp.bfloat16)
        return carry

    lax.fori_loop(0, heads, one_head, 0)


IN_SMEM = pl.BlockSpec(memory_space=pltpu.SMEM)
IN_VMEM = pl.BlockSpec(memory_space=pltpu.VMEM)
KERNEL_VMEM = 48 * 2**20


LANE_GROUP = 128
SPACING = 2


def share_sum_kernel(
    grad_ref, out_ref, core_ref, pair_ref, across_ref, near_ref, near_got_ref, part_ref, piece_ref, send_sem, recv_sem
):
    seq_count, _, half, total = grad_ref.shape
    far_count = lax.axis_size("rows") // 4
    row, place = lax.axis_index("rows"), lax.axis_index("seq")
    core, near, far = lax.rem(row, 2), lax.rem(row // 2, 2), row // 4
    mate = (row + 1 - 2 * core, place)
    close = (row + 2 - 4 * near, place)
    peers = [None] + [
        (lax.rem(far + d, far_count) * 4 + near * 2 + core, place) for d in range(1, far_count)
    ]
    sides = [None] + [(row, lax.rem(place + d, seq_count)) for d in range(1, seq_count)]
    step = 2 * far_count * LANE_GROUP
    wide = far_count * LANE_GROUP
    count = total // step

    barrier = pltpu.get_barrier_semaphore()
    friends = [mate, close] + peers[1:] + sides[1:]
    for friend in friends:
        pl.semaphore_signal(barrier, inc=1, device_id=friend, device_id_type=pl.DeviceIdType.MESH)
    pl.semaphore_wait(barrier, len(friends))

    def copy(chunk, slot, source, target, device):
        return pltpu.make_async_remote_copy(
            src_ref=source,
            dst_ref=target,
            send_sem=send_sem.at[chunk, slot],
            recv_sem=recv_sem.at[chunk, slot],
            device_id=device,
            device_id_type=pl.DeviceIdType.MESH,
        )

    first_side = 1
    near_slot = first_side + seq_count - 1
    first_peer = near_slot + 1
    first_back = first_peer + far_count - 1
    near_back_slot = first_back + far_count - 1
    last_slot = near_back_slot + 1

    def columns(chunk):
        return slice(chunk * step, (chunk + 1) * step)

    def core_copy(chunk):
        return copy(chunk, 0, grad_ref.at[:, 1 - core, :, columns(chunk)], core_ref.at[chunk], mate)

    def side_copy(chunk, d):
        away = lax.rem(place + d, seq_count)
        return copy(chunk, first_side + d - 1, pair_ref.at[chunk, away], across_ref.at[chunk, d - 1], sides[d])

    def near_copy(chunk):
        return copy(chunk, near_slot, near_ref.at[chunk, 1 - near], near_got_ref.at[chunk], close)

    def peer_copy(chunk, d):
        away = lax.rem(far + d, far_count)
        return copy(chunk, first_peer + d - 1, part_ref.at[chunk, away], piece_ref.at[chunk, d - 1], peers[d])

    def own_piece(chunk):
        start = chunk * step + near * wide + far * LANE_GROUP
        return out_ref.at[core, :, pl.ds(pl.multiple_of(start, LANE_GROUP), LANE_GROUP)]

    def back_copy(chunk, d):
        return copy(chunk, first_back + d - 1, own_piece(chunk), own_piece(chunk), peers[d])

    def near_back(chunk):
        start = chunk * step + near * wide
        block = out_ref.at[core, :, pl.ds(pl.multiple_of(start, LANE_GROUP), wide)]
        return copy(chunk, near_back_slot, block, block, close)

    def last_copy(chunk):
        block = out_ref.at[core, :, columns(chunk)]
        return copy(chunk, last_slot, block, block, mate)

    def stage_core(chunk):
        core_copy(chunk).start()

    def stage_side(chunk):
        core_copy(chunk).wait_recv()
        kept = grad_ref[:, core, :, columns(chunk)].astype(jnp.float32)
        pair_ref[chunk] = (kept + core_ref[chunk].astype(jnp.float32)).astype(jnp.bfloat16)
        for d in range(1, seq_count):
            side_copy(chunk, d).start()

    def stage_near(chunk):
        for d in range(1, seq_count):
            side_copy(chunk, d).wait_recv()
        summed = pair_ref[chunk, place].astype(jnp.float32)
        for d in range(1, seq_count):
            summed = summed + across_ref[chunk, d - 1].astype(jnp.float32)
        summed = summed.astype(jnp.bfloat16)
        for side in range(2):
            near_ref[chunk, side] = summed[:, side * wide : (side + 1) * wide]
        near_copy(chunk).start()

    def stage_peer(chunk):
        near_copy(chunk).wait_recv()
        summed = near_ref[chunk, near].astype(jnp.float32) + near_got_ref[chunk].astype(jnp.float32)
        summed = summed.astype(jnp.bfloat16)
        for piece in range(far_count):
            part_ref[chunk, piece] = summed[:, piece * LANE_GROUP : (piece + 1) * LANE_GROUP]
        for d in range(1, far_count):
            peer_copy(chunk, d).start()

    def stage_back(chunk):
        for d in range(1, far_count):
            peer_copy(chunk, d).wait_recv()
        summed = part_ref[chunk, far].astype(jnp.float32)
        for d in range(1, far_count):
            summed = summed + piece_ref[chunk, d - 1].astype(jnp.float32)
        own_piece(chunk)[...] = summed.astype(jnp.bfloat16)
        for d in range(1, far_count):
            back_copy(chunk, d).start()

    def stage_near_back(chunk):
        for d in range(1, far_count):
            back_copy(chunk, d).wait_recv()
        near_back(chunk).start()

    def stage_last(chunk):
        near_back(chunk).wait_recv()
        last_copy(chunk).start()

    def stage_done(chunk):
        last_copy(chunk).wait_recv()
        core_copy(chunk).wait_send()
        for d in range(1, seq_count):
            side_copy(chunk, d).wait_send()
        near_copy(chunk).wait_send()
        for d in range(1, far_count):
            peer_copy(chunk, d).wait_send()
            back_copy(chunk, d).wait_send()
        near_back(chunk).wait_send()
        last_copy(chunk).wait_send()

    for chunk in range(count):
        stage_core(chunk)
    for chunk in range(count):
        stage_side(chunk)
    stages = (stage_near, stage_peer, stage_back, stage_near_back, stage_last, stage_done)
    for tick in range(count + SPACING * (len(stages) - 1)):
        for late, stage in enumerate(stages):
            if 0 <= tick - SPACING * late < count:
                stage(tick - SPACING * late)


def share_summed(packed):
    seq_count = lax.axis_size("seq")
    far_count = lax.axis_size("rows") // 4
    half = packed.shape[0] // (2 * seq_count)
    step = 2 * far_count * LANE_GROUP
    packed = padded_rows(packed, step, 1)
    total = packed.shape[1]
    count = total // step
    slots = 4 + (seq_count - 1) + 2 * (far_count - 1)
    low = jnp.bfloat16
    out = pl.pallas_call(
        share_sum_kernel,
        out_shape=jax.ShapeDtypeStruct((2, half, total), low),
        in_specs=[IN_VMEM],
        out_specs=IN_VMEM,
        scratch_shapes=[
            pltpu.VMEM((count, seq_count, half, step), low),
            pltpu.VMEM((count, seq_count, half, step), low),
            pltpu.VMEM((count, seq_count - 1, half, step), low),
            pltpu.VMEM((count, 2, half, step // 2), low),
            pltpu.VMEM((count, half, step // 2), low),
            pltpu.VMEM((count, far_count, half, LANE_GROUP), low),
            pltpu.VMEM((count, far_count - 1, half, LANE_GROUP), low),
            pltpu.SemaphoreType.DMA((count, slots)),
            pltpu.SemaphoreType.DMA((count, slots)),
        ],
        compiler_params=pltpu.CompilerParams(
            collective_id=0, has_side_effects=True, vmem_limit_bytes=KERNEL_VMEM
        ),
        name="share_sum",
    )(packed.reshape(seq_count, 2, half, total))
    return out.reshape(2 * half, total)


def attend_forward(queries, pairs_t, heads, causal, query_seg, key_seg):
    width, tokens = queries.shape
    total_keys = pairs_t.shape[1]
    pairs = heads * tokens * total_keys
    return pl.pallas_call(
        functools.partial(attend_kernel, heads, causal),
        out_shape=(
            jax.ShapeDtypeStruct((width, tokens), jnp.bfloat16),
            jax.ShapeDtypeStruct((heads, 1, tokens), jnp.float32),
        ),
        in_specs=[IN_SMEM] + [IN_VMEM] * 4,
        out_specs=(IN_VMEM, IN_VMEM),
        scratch_shapes=[pltpu.VMEM((SEG_ROWS, total_keys), jnp.bfloat16)],
        compiler_params=pltpu.CompilerParams(vmem_limit_bytes=KERNEL_VMEM),
        cost_estimate=pl.CostEstimate(
            flops=pairs * 600, bytes_accessed=4 * width * total_keys, transcendentals=pairs
        ),
        name="attend_fwd",
    )(lax.axis_index("seq").reshape(1), queries, pairs_t, query_seg[None], key_seg[None])


def attend_back(queries, pairs_t, grads, outs, totals, heads, causal, query_seg, key_seg):
    width, tokens = queries.shape
    total_keys = pairs_t.shape[1]
    pairs = heads * tokens * total_keys
    size = width // heads
    return pl.pallas_call(
        functools.partial(attend_back_kernel, heads, causal),
        out_shape=(
            jax.ShapeDtypeStruct((width, tokens), jnp.bfloat16),
            jax.ShapeDtypeStruct((2 * width, total_keys), jnp.bfloat16),
        ),
        in_specs=[IN_SMEM] + [IN_VMEM] * 7,
        out_specs=(IN_VMEM, IN_VMEM),
        scratch_shapes=[
            pltpu.VMEM((SEG_ROWS, total_keys), jnp.bfloat16),
            pltpu.VMEM((size, total_keys), jnp.float32),
            pltpu.VMEM((size, total_keys), jnp.float32),
        ],
        compiler_params=pltpu.CompilerParams(vmem_limit_bytes=KERNEL_VMEM),
        cost_estimate=pl.CostEstimate(
            flops=pairs * 1500, bytes_accessed=8 * width * total_keys, transcendentals=pairs
        ),
        name="attend_bwd",
    )(
        lax.axis_index("seq").reshape(1), queries, pairs_t, grads, outs, totals,
        query_seg[None], key_seg[None],
    )


RIM = 16
ROW_TILE = 64


def row_tiles(extent, tile):
    return [(low, min(low + tile, extent)) for low in range(0, extent, tile)]


def halves_of(extent):
    middle = -(-extent // 32) * 16
    return [(0, middle), (middle, extent)]


def group_lanes(group):
    return pl.ds(pl.multiple_of(group * 128, 128), 128)


def wide_rows(column, width=128):
    return jnp.broadcast_to(column, (column.shape[0], width))


def loop_rows(extent, tile, body):
    def step(k, carry):
        body(pl.ds(pl.multiple_of(k * tile, tile), tile))
        return carry

    lax.fori_loop(0, extent // tile, step, 0)


def rows_normed(values):
    centre = values - jnp.mean(values, axis=-1, keepdims=True)
    inverse = lax.rsqrt(jnp.mean(centre * centre, axis=-1, keepdims=True) + EPSILON)
    return centre * inverse, inverse


def rows_norm_back(normed, inverse, gain_vec, upstream):
    scaled = upstream * gain_vec
    return inverse * (
        scaled
        - jnp.mean(scaled, axis=-1, keepdims=True)
        - normed * jnp.mean(scaled * normed, axis=-1, keepdims=True)
    )


def taps_forward(source_ref, first_row, since, lanes, low, high, weights):
    result = None
    for offset, weight in enumerate(weights):
        start = first_row + low - offset
        window = source_ref[start : start + high - low, lanes]
        if offset:
            window = jnp.where(since >= offset, window, 0.0)
        term = window * weight
        result = term if result is None else result + term
    return result


def conv_fwd_kernel(
    h1_ref, a2_ref, rim_ref, since_ref, tl_ref, tr_ref, tm_ref, mgain_ref, gain_ref, pl_ref, pr_ref, pm_ref,
    cl_ref, cr_ref, cm_ref, h2_ref, a3_ref,
    ext_ref, wide_ref, cle_ref, cre_ref, up_ref, mixed_ref,
):
    tokens, width = h1_ref.shape
    total = tokens + RIM
    narrow = pr_ref.shape[1]
    ext_ref[0:RIM, :] = jnp.zeros((RIM, width), jnp.float32)
    ext_ref[RIM : 2 * RIM, :] = rim_ref[...].astype(jnp.float32)
    ext_ref[2 * RIM :, :] = a2_ref[...].astype(jnp.float32)
    wide_ref[...] = wide_rows(since_ref[...])

    def first_convs(group, carry):
        lanes = group_lanes(group)
        left = [tl_ref[j : j + 1, lanes] for j in range(tl_ref.shape[0])]
        right = [tr_ref[j : j + 1, lanes] for j in range(tr_ref.shape[0])]
        for low, high in row_tiles(total, ROW_TILE):
            since = wide_ref[low:high, :]
            cle_ref[low:high, lanes] = taps_forward(ext_ref, RIM, since, lanes, low, high, left).astype(jnp.bfloat16)
            cre_ref[low:high, lanes] = taps_forward(ext_ref, RIM, since, lanes, low, high, right).astype(jnp.bfloat16)
        return carry

    lax.fori_loop(0, width // 128, first_convs, 0)
    cl_ref[...] = cle_ref[RIM:, :]
    cr_ref[...] = cre_ref[RIM:, :]
    for low, high in halves_of(total):
        up_ref[low:high, :] = nn_dot(cle_ref[low:high, :], pl_ref[...])
        mixed_ref[low:high, :narrow] = nn_dot(cre_ref[low:high, :], pr_ref[...])

    def merge_rows(rows):
        pre = up_ref[rows, :]
        merged = pre / (1.0 + jnp.exp(-pre))
        merged = jnp.concatenate([merged[:, :narrow] + mixed_ref[rows, :narrow], merged[:, narrow:]], 1)
        normed, _ = rows_normed(merged)
        mixed_ref[rows, :] = (normed * mgain_ref[...]).astype(jnp.bfloat16).astype(jnp.float32)

    loop_rows(total, 16, merge_rows)

    def mid_conv(group, carry):
        lanes = group_lanes(group)
        weights = [tm_ref[j : j + 1, lanes] for j in range(tm_ref.shape[0])]
        for low, high in row_tiles(tokens, ROW_TILE):
            since = wide_ref[RIM + low : RIM + high, :]
            cm_ref[low:high, lanes] = taps_forward(mixed_ref, RIM, since, lanes, low, high, weights).astype(jnp.bfloat16)
        return carry

    lax.fori_loop(0, mixed_ref.shape[1] // 128, mid_conv, 0)
    for low, high in halves_of(tokens):
        h2_ref[low:high, :] = h1_ref[low:high, :] + nn_dot(cm_ref[low:high, :], pm_ref[...])

    def norm_rows(rows):
        normed, _ = rows_normed(h2_ref[rows, :])
        a3_ref[rows, :] = (normed * gain_ref[...]).astype(jnp.bfloat16)

    loop_rows(tokens, 32, norm_rows)


def conv_forward(h1, a2, rim, since, taps_l, taps_r, taps_m, mid_gain, gain, proj_left, proj_right, proj_mid):
    tokens, width = h1.shape
    wide = proj_left.shape[1]
    total = tokens + RIM
    low, full = jnp.bfloat16, jnp.float32
    return pl.pallas_call(
        conv_fwd_kernel,
        out_shape=(
            jax.ShapeDtypeStruct((tokens, width), low),
            jax.ShapeDtypeStruct((tokens, width), low),
            jax.ShapeDtypeStruct((tokens, wide), low),
            jax.ShapeDtypeStruct((tokens, width), full),
            jax.ShapeDtypeStruct((tokens, width), low),
        ),
        in_specs=[IN_VMEM] * 12,
        out_specs=(IN_VMEM,) * 5,
        scratch_shapes=[
            pltpu.VMEM((total + RIM, width), full),
            pltpu.VMEM((total, 128), jnp.int32),
            pltpu.VMEM((total, width), low),
            pltpu.VMEM((total, width), low),
            pltpu.VMEM((total, wide), full),
            pltpu.VMEM((total, wide), full),
        ],
        compiler_params=pltpu.CompilerParams(vmem_limit_bytes=KERNEL_VMEM),
        cost_estimate=pl.CostEstimate(
            flops=tokens * width * wide * 20, bytes_accessed=tokens * width * 16, transcendentals=tokens * wide
        ),
        name="conv_fwd",
    )(h1, a2, rim, since, taps_l, taps_r, taps_m, mid_gain, gain, proj_left, proj_right, proj_mid)


def folded(values):
    return jnp.sum(values.reshape(-1, 8, values.shape[-1]), axis=0)


def taps_back(grad_ref, value, left, lanes, low, high, weights, result, sums):
    for offset, weight in enumerate(weights):
        window = grad_ref[low + offset : high + offset, lanes]
        if offset:
            window = jnp.where(left >= offset, window, 0.0)
        term = window * weight
        result = term if result is None else result + term
        if value is not None:
            product = folded(window * value)
            sums[offset] = product if sums[offset] is None else sums[offset] + product
    return result


def conv_bwd_kernel(
    g2_ref, brim_ref, cl_ref, clrim_ref, cr_ref, crrim_ref, cm_ref, a2_ref, h1_ref, left_ref,
    tl_ref, tr_ref, tm_ref, mgain_ref, gain_ref, pl_ref, pr_ref, pm_ref,
    g1_ref, dw_ref, dtl_ref, dtr_ref, dtm_ref, dmgain_ref, dgain_ref,
    bext_ref, cle_ref, cre_ref, wide_ref, grad_ref, up_ref, back_ref, normed_ref, inv_ref, dpl_ref, dpr_ref, a2f_ref,
):
    tokens, width = g2_ref.shape
    total = tokens + RIM
    wide, narrow = pl_ref.shape[1], pr_ref.shape[1]
    bext_ref[:tokens, :] = g2_ref[...].astype(jnp.bfloat16)
    bext_ref[tokens:, :] = brim_ref[...]
    cle_ref[:tokens, :] = cl_ref[...]
    cle_ref[tokens:, :] = clrim_ref[...]
    cre_ref[:tokens, :] = cr_ref[...]
    cre_ref[tokens:, :] = crrim_ref[...]
    a2f_ref[...] = a2_ref[...].astype(jnp.float32)
    wide_ref[...] = wide_rows(left_ref[...])
    grad_ref[total:, :] = jnp.zeros((RIM, wide), jnp.float32)
    dw_ref[:, :wide] = tn_dot(bext_ref[:tokens, :], cm_ref[...]).astype(jnp.bfloat16)
    for low, high in halves_of(total):
        grad_ref[low:high, :] = nt_dot(bext_ref[low:high, :], pm_ref[...])
        up_ref[low:high, :] = nn_dot(cle_ref[low:high, :], pl_ref[...])
        back_ref[low:high, :narrow] = nn_dot(cre_ref[low:high, :], pr_ref[...])

    def merge_rows(rows):
        pre = up_ref[rows, :]
        merged = pre / (1.0 + jnp.exp(-pre))
        merged = jnp.concatenate([merged[:, :narrow] + back_ref[rows, :narrow], merged[:, narrow:]], 1)
        normed, inverse = rows_normed(merged)
        normed_ref[rows, :] = normed
        inv_ref[rows, :] = wide_rows(inverse)

    loop_rows(total, 16, merge_rows)

    def mid_back(group, carry):
        lanes = group_lanes(group)
        weights = [tm_ref[j : j + 1, lanes] for j in range(tm_ref.shape[0])]
        sums = [None] * len(weights)
        gain_vec = mgain_ref[:, lanes]
        for low, high in row_tiles(total, ROW_TILE):
            value = None
            if high <= tokens:
                value = (normed_ref[low:high, lanes] * gain_vec).astype(jnp.bfloat16).astype(jnp.float32)
            back_ref[low:high, lanes] = taps_back(
                grad_ref, value, wide_ref[low:high, :], lanes, low, high, weights, None, sums
            )
        for j, piece in enumerate(sums):
            dtm_ref[j : j + 1, lanes] = jnp.sum(piece, axis=0, keepdims=True)
        return carry

    lax.fori_loop(0, wide // 128, mid_back, 0)

    def merge_back(rows):
        pre = up_ref[rows, :]
        normed = normed_ref[rows, :]
        d_merged = rows_norm_back(normed, inv_ref[rows, :][:, :1], mgain_ref[...], back_ref[rows, :])
        sigma = 1.0 / (1.0 + jnp.exp(-pre))
        dpl_ref[rows, :] = (d_merged * (sigma * (1.0 + pre * (1.0 - sigma)))).astype(jnp.bfloat16)
        dpr_ref[rows, :] = d_merged[:, :narrow].astype(jnp.bfloat16)

    loop_rows(total, 16, merge_back)
    gain_sum = jnp.zeros((8, wide), jnp.float32)

    def gain_rows(k, held):
        rows = pl.ds(pl.multiple_of(k * 16, 16), 16)
        return held + folded(back_ref[rows, :] * normed_ref[rows, :])

    gain_sum = lax.fori_loop(0, tokens // 16, gain_rows, gain_sum)
    dmgain_ref[...] = jnp.sum(gain_sum, axis=0, keepdims=True)
    dw_ref[:, wide : 2 * wide] = tn_dot(cle_ref[:tokens, :], dpl_ref[:tokens, :]).astype(jnp.bfloat16)
    dw_ref[:, 2 * wide :] = tn_dot(cre_ref[:tokens, :], dpr_ref[:tokens, :]).astype(jnp.bfloat16)
    for low, high in halves_of(total):
        grad_ref[low:high, :width] = nt_dot(dpl_ref[low:high, :], pl_ref[...])
        grad_ref[low:high, width : 2 * width] = nt_dot(dpr_ref[low:high, :], pr_ref[...])

    def first_back(group, carry):
        lanes = group_lanes(group)
        other = group_lanes(group + width // 128)
        weights_l = [tl_ref[j : j + 1, lanes] for j in range(tl_ref.shape[0])]
        weights_r = [tr_ref[j : j + 1, lanes] for j in range(tr_ref.shape[0])]
        sums_l = [None] * len(weights_l)
        sums_r = [None] * len(weights_r)
        for low, high in row_tiles(tokens, ROW_TILE):
            left = wide_ref[low:high, :]
            value = a2f_ref[low:high, lanes]
            held = taps_back(grad_ref, value, left, lanes, low, high, weights_l, None, sums_l)
            held = taps_back(grad_ref, value, left, other, low, high, weights_r, held, sums_r)
            back_ref[low:high, lanes] = held
        for j, piece in enumerate(sums_l):
            dtl_ref[j : j + 1, lanes] = jnp.sum(piece, axis=0, keepdims=True)
        for j, piece in enumerate(sums_r):
            dtr_ref[j : j + 1, lanes] = jnp.sum(piece, axis=0, keepdims=True)
        return carry

    lax.fori_loop(0, width // 128, first_back, 0)

    def finish(k, held):
        rows = pl.ds(pl.multiple_of(k * 32, 32), 32)
        normed, inverse = rows_normed(h1_ref[rows, :])
        upstream = back_ref[rows, :width]
        g1_ref[rows, :] = g2_ref[rows, :] + rows_norm_back(normed, inverse, gain_ref[...], upstream)
        return held + folded(upstream * normed)

    gain_sum = lax.fori_loop(0, tokens // 32, finish, jnp.zeros((8, width), jnp.float32))
    dgain_ref[...] = jnp.sum(gain_sum, axis=0, keepdims=True)


def conv_back(
    g2, brim, c_l, c_r, rims, c_m, a2, h1, left, taps_l, taps_r, taps_m, mid_gain, gain, proj_left, proj_right, proj_mid
):
    tokens, width = g2.shape
    wide, narrow = proj_left.shape[1], proj_right.shape[1]
    total = tokens + RIM
    low, full = jnp.bfloat16, jnp.float32
    return pl.pallas_call(
        conv_bwd_kernel,
        out_shape=(
            jax.ShapeDtypeStruct((tokens, width), full),
            jax.ShapeDtypeStruct((width, 2 * wide + narrow), low),
            jax.ShapeDtypeStruct(taps_l.shape, full),
            jax.ShapeDtypeStruct(taps_r.shape, full),
            jax.ShapeDtypeStruct(taps_m.shape, full),
            jax.ShapeDtypeStruct((1, wide), full),
            jax.ShapeDtypeStruct((1, width), full),
        ),
        in_specs=[IN_VMEM] * 18,
        out_specs=(IN_VMEM,) * 7,
        scratch_shapes=[
            pltpu.VMEM((total, width), low),
            pltpu.VMEM((total, width), low),
            pltpu.VMEM((total, width), low),
            pltpu.VMEM((total, 128), jnp.int32),
            pltpu.VMEM((total + RIM, wide), full),
            pltpu.VMEM((total, wide), full),
            pltpu.VMEM((total, wide), full),
            pltpu.VMEM((total, wide), full),
            pltpu.VMEM((total, 128), full),
            pltpu.VMEM((total, wide), low),
            pltpu.VMEM((total, narrow), low),
            pltpu.VMEM((tokens, width), full),
        ],
        compiler_params=pltpu.CompilerParams(vmem_limit_bytes=KERNEL_VMEM),
        cost_estimate=pl.CostEstimate(
            flops=tokens * width * wide * 40, bytes_accessed=tokens * width * 40, transcendentals=tokens * wide
        ),
        name="conv_bwd",
    )(
        g2, brim, c_l, rims[:, :width], c_r, rims[:, width:], c_m, a2, h1, left,
        taps_l, taps_r, taps_m, mid_gain, gain, proj_left, proj_right, proj_mid,
    )


def segment_reach(seg_row):
    length = seg_row.shape[0]
    first = jnp.sum(seg_row == 0)
    second = first + jnp.sum(seg_row == 1)
    spots = jnp.arange(length, dtype=jnp.int32)
    start = jnp.where(seg_row == 0, 0, jnp.where(seg_row == 1, first, second))
    stop = jnp.where(seg_row == 0, first, jnp.where(seg_row == 1, second, length))
    return spots - start, stop - 1 - spots


def turned_dot(weight, values):
    return jnp.einsum("kn,tk->nt", weight, values, preferred_element_type=jnp.float32)


def out_dot(turned, weight):
    return jnp.einsum("nt,nk->tk", turned, weight, preferred_element_type=jnp.float32)


def weight_dot(values, turned):
    return jnp.einsum("tk,nt->kn", values, turned, preferred_element_type=jnp.float32)


def out_weight_dot(turned, grads_in):
    return jnp.einsum("nt,tk->kn", turned, grads_in, preferred_element_type=jnp.float32)


def turned_back(grads_in, weight):
    return jnp.einsum("tk,nk->nt", grads_in, weight, preferred_element_type=jnp.float32)


def input_back(turned, weight):
    return jnp.einsum("nt,kn->tk", turned, weight, preferred_element_type=jnp.float32)


def self_attend(normed, normed_row, weight, head_count, own_seg, seg_row):
    model_width = normed.shape[1]
    queries = turned_dot(weight[:, :model_width], normed).astype(jnp.bfloat16)
    pairs = turned_dot(weight[:, model_width:], normed_row).astype(jnp.bfloat16)
    att_out, totals = attend_forward(queries, pairs, head_count, True, own_seg, seg_row)
    return (att_out, totals, queries, pairs, normed_row)


def self_back(normed, weight, grad_att, kept, head_count, own_seg, seg_row):
    att_out, totals, queries, pairs, normed_row = kept
    model_width = normed.shape[1]
    d_query, d_pairs = attend_back(
        queries, pairs, grad_att, att_out, totals, head_count, True, own_seg, seg_row
    )
    d_weight = jnp.concatenate([weight_dot(normed, d_query), weight_dot(normed_row, d_pairs)], 1)
    d_normed = input_back(d_query, weight[:, :model_width]) + row_sum_owned(
        input_back(d_pairs, weight[:, model_width:]).astype(jnp.bfloat16)
    )
    return (d_normed, d_weight)


def local(
    hidden_in,
    memory,
    grad_out,
    seg_ids,
    mem_seg_ids,
    gains,
    qkv_first,
    query_cross,
    kv_cross,
    out_first,
    taps_left,
    proj_left,
    taps_right,
    proj_right,
    mid_gain,
    taps_mid,
    proj_mid,
    qkv_second,
    out_second,
    query_last,
    kv_last,
    out_last,
    ffn_up,
    ffn_down,
):
    shards = (
        gains,
        qkv_first,
        query_cross,
        kv_cross,
        out_first,
        taps_left,
        proj_left,
        taps_right,
        proj_right,
        mid_gain,
        taps_mid,
        proj_mid,
        qkv_second,
        out_second,
        query_last,
        kv_last,
        out_last,
        ffn_up,
        ffn_down,
    )
    shard_dims = (1, 0, 0, 0, 1, 1, 0, 1, 0, 0, 1, 1, 0, 0, 0, 0, 0, 0, 1)
    small = (0, 5, 7, 9, 10)
    fulls = [None] * len(shards)
    row_inputs = gathered(hidden_in[0])
    found, earlier = small_gather([shards[k] for k in small], [shard_dims[k] for k in small], row_inputs)
    for k, whole in zip(small, found):
        fulls[k] = whole
    for group in ((1,), (2, 3), (4, 6, 8, 11)):
        if group == (2, 3):
            mem_rows = gathered(after(memory[0], earlier)[0])
        found, arrived = group_gather([shards[k] for k in group], [shard_dims[k] for k in group], earlier)
        if group == (1,):
            earlier = arrived
        for k, whole in zip(group, found):
            fulls[k] = whole
    (
        gains,
        qkv_first,
        query_cross,
        kv_cross,
        out_first,
        taps_left,
        proj_left,
        taps_right,
        proj_right,
        mid_gain,
        taps_mid,
        proj_mid,
        *_,
    ) = fulls
    inputs = hidden_in[0].astype(jnp.float32)
    seg_row = seg_ids[0]
    mem_seg = mem_seg_ids[0]
    tok_count, model_width = inputs.shape
    row_start = lax.axis_index("seq") * tok_count
    own_seg = lax.dynamic_slice_in_dim(seg_row, row_start, tok_count)
    since, left = segment_reach(seg_row)
    since = lax.dynamic_slice_in_dim(jnp.pad(since, (RIM, 0)), row_start, tok_count + RIM)[:, None]
    left = lax.dynamic_slice_in_dim(jnp.pad(left, (0, RIM)), row_start, tok_count + RIM)[:, None]
    gain_rows = gains.astype(jnp.float32)
    mid_gain_f = mid_gain.astype(jnp.float32)
    left_taps = taps_left.astype(jnp.float32)
    right_taps = taps_right.astype(jnp.float32)
    mid_taps = taps_mid.astype(jnp.float32)
    pairs_b = turned_dot(kv_cross, mem_rows).astype(jnp.bfloat16)
    normed_a = layer_norm(inputs, gain_rows[0]).astype(jnp.bfloat16)
    normed_row = layer_norm(row_inputs.astype(jnp.float32), gain_rows[0]).astype(jnp.bfloat16)
    kept_a = self_attend(normed_a, normed_row, qkv_first, H_SELF, own_seg, seg_row)
    query_b = turned_dot(query_cross, normed_a).astype(jnp.bfloat16)
    out_b, total_b = attend_forward(query_b, pairs_b, H_CROSS, False, own_seg, mem_seg)
    hidden_b = (
        inputs
        + out_dot(kept_a[0], out_first[:model_width])
        + out_dot(out_b, out_first[model_width:])
    )
    normed_c = layer_norm(hidden_b, gain_rows[1]).astype(jnp.bfloat16)
    (qkv_second, out_second, query_last, kv_last, out_last), _ = group_gather(
        shards[12:17], shard_dims[12:17], hidden_b
    )
    conv_l, conv_r, conv_m, hidden_c, normed_d = conv_forward(
        hidden_b,
        normed_c,
        passed_along(normed_c[tok_count - RIM :], "seq", 1),
        since,
        left_taps,
        right_taps,
        mid_taps,
        mid_gain_f[None],
        gain_rows[2:3],
        proj_left,
        proj_right,
        proj_mid,
    )
    (ffn_up, ffn_down), _ = group_gather(shards[17:], shard_dims[17:], hidden_c)
    pairs_d = turned_dot(kv_last, mem_rows).astype(jnp.bfloat16)
    conv_rims = passed_along(jnp.concatenate([conv_l[:RIM], conv_r[:RIM]], 1), "seq", -1)
    kept_c = self_attend(normed_d, gathered(normed_d), qkv_second, H_CROSS, own_seg, seg_row)
    att_c = kept_c[0]
    hidden_d = hidden_c + out_dot(att_c, out_second)
    normed_e = layer_norm(hidden_d, gain_rows[3]).astype(jnp.bfloat16)
    query_d = turned_dot(query_last, normed_e).astype(jnp.bfloat16)
    att_d, total_d = attend_forward(query_d, pairs_d, H_CROSS, False, own_seg, mem_seg)
    hidden_e = hidden_d + out_dot(att_d, out_last)
    normed_f = layer_norm(hidden_e, gain_rows[4]).astype(jnp.bfloat16)
    up_pre = plain_dot(normed_f, ffn_up)
    activ_low = jax.nn.silu(up_pre).astype(jnp.bfloat16)
    result = hidden_e + plain_dot(activ_low, ffn_down)
    grad_now = grad_out[0].astype(jnp.float32)
    branch = grad_now.astype(jnp.bfloat16)
    d_ffn_down = left_dot(branch, activ_low)
    d_up = (right_dot(branch, ffn_down) * swish_slope(up_pre)).astype(jnp.bfloat16)
    d_ffn_up = left_dot(normed_f, d_up)
    part_a = offload_rows(jnp.concatenate([d_ffn_up, d_ffn_down], 1).astype(jnp.bfloat16))
    d_hidden, g_five = norm_back(hidden_e, gain_rows[4], right_dot(d_up, ffn_up))
    grad_now = grad_now + d_hidden
    branch = grad_now.astype(jnp.bfloat16)
    d_out_last = out_weight_dot(att_d, branch)
    d_att = turned_back(branch, out_last).astype(jnp.bfloat16)
    dq_d, dkv_d = attend_back(
        query_d, pairs_d, d_att, att_d, total_d, H_CROSS, False, own_seg, mem_seg
    )
    d_query_last = weight_dot(normed_e, dq_d)
    d_hidden, g_four = norm_back(hidden_d, gain_rows[3], input_back(dq_d, query_last))
    grad_now = grad_now + d_hidden
    branch = grad_now.astype(jnp.bfloat16)
    d_out_second = out_weight_dot(att_c, branch)
    d_att = turned_back(branch, out_second).astype(jnp.bfloat16)
    d_normed, d_qkv_second = self_back(
        normed_d, qkv_second, d_att, kept_c, H_CROSS, own_seg, seg_row
    )
    d_kv_last = weight_dot(mem_rows, dkv_d)
    part_b = offload_rows(
        jnp.concatenate([d_out_last.T, d_query_last, d_kv_last, d_qkv_second, d_out_second.T], 1).astype(jnp.bfloat16)
    )
    d_hidden, g_three = norm_back(hidden_c, gain_rows[2], d_normed)
    grad_now = grad_now + d_hidden
    branch = grad_now.astype(jnp.bfloat16)
    grad_now, part_a = after(grad_now, part_a)
    part_a = offload_seq(part_a)
    grad_now, d_projections, d_taps_left, d_taps_right, d_taps_mid, d_mid_gain, g_two = conv_back(
        grad_now,
        passed_along(branch[:RIM], "seq", -1),
        conv_l,
        conv_r,
        conv_rims,
        conv_m,
        normed_c,
        hidden_b,
        left,
        left_taps,
        right_taps,
        mid_taps,
        mid_gain_f[None],
        gain_rows[1:2],
        proj_left,
        proj_right,
        proj_mid,
    )
    d_mid_gain, g_two = d_mid_gain[0], g_two[0]
    branch = grad_now.astype(jnp.bfloat16)
    d_out_first = jnp.concatenate(
        [out_weight_dot(kept_a[0], branch), out_weight_dot(out_b, branch)], 1
    )
    branch, (part_a, part_b) = after(branch, (part_a, part_b))
    part_a = offload_back(part_a)
    part_b = offload_seq(part_b)
    d_att_a = turned_back(branch, out_first[:model_width]).astype(jnp.bfloat16)
    d_att_b = turned_back(branch, out_first[model_width:]).astype(jnp.bfloat16)
    dq_b, dkv_b = attend_back(
        query_b, pairs_b, d_att_b, out_b, total_b, H_CROSS, False, own_seg, mem_seg
    )
    d_query_cross = weight_dot(normed_a, dq_b)
    d_normed, d_qkv_first = self_back(
        normed_a, qkv_first, d_att_a, kept_a, H_SELF, own_seg, seg_row
    )
    d_normed, part_b = after(d_normed, part_b)
    part_b = offload_back(part_b)
    d_normed = d_normed + input_back(dq_b, query_cross)
    d_hidden, g_one = norm_back(inputs, gain_rows[0], d_normed)
    grad_in = grad_now + d_hidden
    grad_mem = row_sum_owned(
        (input_back(dkv_b, kv_cross) + input_back(dkv_d, kv_last)).astype(jnp.bfloat16)
    )
    d_kv_cross = weight_dot(mem_rows, dkv_b)
    d_gains = jnp.stack([g_one, g_two, g_three, g_four, g_five], 0)
    wide, narrow = proj_left.shape[1], proj_right.shape[1]
    width = model_width // lax.axis_size("seq")
    small_grads = (d_gains, d_taps_left, d_taps_right, d_mid_gain, d_taps_mid)
    last = [d_projections] + [
        piece.astype(jnp.bfloat16) for piece in (d_out_first, d_kv_cross, d_query_cross, d_qkv_first)
    ]
    last.append(small_columns(small_grads, width))
    part_c = share_summed(jnp.concatenate(last, 1))
    shares = [None] * len(shards)
    up = ffn_up.shape[1]
    for part, group, sizes in (
        (part_a, (17, 18), (up, up)),
        (
            part_b,
            (16, 14, 15, 12, 13),
            (model_width, model_width, 2 * model_width, 3 * model_width, model_width),
        ),
        (
            part_c,
            (11, 6, 8, 4, 3, 2, 1),
            (wide, wide, narrow, 2 * model_width, 2 * model_width, model_width, 3 * model_width),
        ),
    ):
        offset = 0
        for k, size in zip(group, sizes):
            piece = part[:, offset : offset + size].astype(jnp.float32)
            shares[k] = piece if shard_dims[k] == 0 else piece.T
            offset = offset + size
    parts = small_shares(part_c[:, offset : offset + 128].astype(jnp.float32), small_grads, width)
    for k, piece in zip(small, parts):
        shares[k] = piece
    return (
        result.astype(jnp.bfloat16)[None],
        grad_in[None],
        grad_mem[None],
        shares[0],
        shares[1],
        shares[2],
        shares[3],
        shares[4],
        shares[5],
        shares[6],
        shares[7],
        shares[8],
        shares[9],
        shares[10],
        shares[11],
        shares[12],
        shares[13],
        shares[14],
        shares[15],
        shares[16],
        shares[17],
        shares[18],
    )


def solution(mesh):
    placed = (
        P("rows", "seq", None),
        P("rows", "seq", None),
        P("rows", "seq", None),
        P("rows", None),
        P("rows", None),
        P(None, "seq"),
        P("seq", None),
        P("seq", None),
        P("seq", None),
        P(None, "seq"),
        P(None, "seq"),
        P("seq", None),
        P(None, "seq"),
        P("seq", None),
        P("seq"),
        P(None, "seq"),
        P(None, "seq"),
        P("seq", None),
        P("seq", None),
        P("seq", None),
        P("seq", None),
        P("seq", None),
        P("seq", None),
        P(None, "seq"),
    )
    return jax.shard_map(
        local,
        mesh=mesh,
        in_specs=placed,
        out_specs=(
            P("rows", "seq", None),
            P("rows", "seq", None),
            P("rows", "seq", None),
            P(None, "seq"),
            P("seq", None),
            P("seq", None),
            P("seq", None),
            P(None, "seq"),
            P(None, "seq"),
            P("seq", None),
            P(None, "seq"),
            P("seq", None),
            P("seq"),
            P(None, "seq"),
            P(None, "seq"),
            P("seq", None),
            P("seq", None),
            P("seq", None),
            P("seq", None),
            P("seq", None),
            P("seq", None),
            P(None, "seq"),
        ),
        check_vma=False,
    )
```

time: 2080 us -> 662 us (0.32)
  local copies, waits for them, and re-layouts: 743 us -> 87.2 us
  blocking collectives: 584 us -> 0 us
  matrix products: 350 us -> 75.3 us
  Pallas kernels: 0 us -> 248 us
  waiting for transfers between devices: 243 us -> 78.2 us
  starting transfers between devices: 9.88 us -> 100 us
  other arithmetic: 100 us -> 43 us
    unnamed x1 -> x0, blocking collectives: 482 us -> none
    unnamed x645 -> x370, local copies, waits for them, and re-layouts: 503 us -> 36.8 us
    pallas_call x0 -> x11, Pallas kernels: none -> 248 us  [the longest x1 82 us: share_summed(): pl.pallas_call(share_sum_kernel, out_shape=jax.ShapeDtypeStruct((2, half,...]
    dot_general x44 -> x36, matrix products: 258 us -> 58.1 us  [the longest x8 19.1 us: weight_dot(): jnp.einsum('tk,nt->kn', values, turned, preferred_element_type=jnp.float32)]
    reshape x38 -> x22, local copies, waits for them, and re-layouts: 159 us -> 2.34 us  [the longest x2 1.46 us: flat_half(): return jnp.swapaxes(blocks, 0, 1).reshape(width // 2, -1)]
    unnamed x19 -> x6, waiting for transfers between devices: 151 us -> 0.1 us
    all_gather x12 -> x0, blocking collectives: 103 us -> none  [the longest x1 15.2 us: local(): lax.all_gather(query_last, 'seq', axis=0, tiled=True)]
    ppermute x0 -> x17, starting transfers between devices: none -> 68 us  [the longest x3 56.2 us: halved_sum(): lax.ppermute(sent, axis, [(i, i ^ bit) for i in range(lax.axis_size(axis))])]
  transfers between devices with their start and end apart: 21 -> 26, of which waited for: 8 -> 7; matrix products, arithmetic and copies ran while one was open for 23% -> 24% of each run, Pallas kernels for 0% -> 38%
where the time goes in v1:
time: 662 us; the launch traced here: 651 us
  Pallas kernels  248 us (37%)
  starting transfers between devices  100 us (15%)
  local copies, waits for them, and re-layouts  87.2 us (13%)
  waiting for transfers between devices  78.2 us (12%)
  matrix products  75.3 us (11%)
  other arithmetic  43 us (6%)
  between operations  18.4 us (3%)
    pallas_call x1, Pallas kernels, share_summed(): pl.pallas_call(share_sum_kernel, out_shape=jax.ShapeDtypeStruct((2, half,...  82 us
    ppermute x3, starting transfers between devices, halved_sum(): lax.ppermute(sent, axis, [(i, i ^ bit) for i in range(lax.axis_size(axis))])  56.2 us
    pallas_call x4, Pallas kernels, attend_back(): pl.pallas_call(functools.partial(attend_back_kernel, heads, causal), out_...  55.4 us
    pallas_call x4, Pallas kernels, attend_forward(): pl.pallas_call(functools.partial(attend_kernel, heads, causal), out_shape...  48.8 us
    ppermute x9, waiting for transfers between devices, rotated(): lax.ppermute(block, axis, [((i + distance) % size, i) for i in range(size)])  48.6 us
    pallas_call x1, Pallas kernels, conv_back(): pl.pallas_call(conv_bwd_kernel, out_shape=(jax.ShapeDtypeStruct((tokens,...  37.9 us
    unnamed x370, local copies, waits for them, and re-layouts  36.8 us
    ppermute x3, starting transfers between devices, passed_along(): return lax.ppermute(block, axis, route)  31.8 us
  transfers between devices with their start and end apart: 26, of which 7 were waited for; matrix products, arithmetic and copies ran while one was open for 24% of the time, Pallas kernels for 38%

profile of v1, /device:TPU:0, one launch (start us, length us, event | category | flops | bytes accessed | tf_op | source)
XLA Modules:
  0.0 650.7 jit_solution(7016709352109941570)
XLA Ops:
  9.3 2.9 collective-permute-start
  41.3 24.2 %collective-permute-done.3 = bf16[80,128]{1,0:T(8,128)(2,1)S(1)} collective-permute-done((bf16[80,128]{1,0:T(8,128)(2,1)S(1)}, bf16[80,128]{1,0:T(8,128)(2,1)S(1)}, u32[]{:S(2)}, u32[]{:S(2)}) %collective-permute-start.3) | collective-permute-done | bytes 20512 | tf_op jit(solution)/shard_map/ppermute | solution.py:24
  74.9 22.1 %attend_fwd.4 = (bf16[512,640]{1,0:T(8,128)(2,1)S(1)}, f32[16,1,640]{2,1,0:T(1,128)S(1)}) custom-call(s32[1]{0:T(128)} %bitcast.1.place_ref, bf16[512,640]{1,0:T(8,128)(2,1)S(1)} %convolution_convert_fusion.17.qt_ref, bf16[1024,1280]{1,0:T(8,128)(2,1)S(1)} %convolution_convert_fusion.1.pair_ref, s32[1,640]{1,0:T(1,128)S(1)} %constant_dynamic-slice_fusion.11.qseg_ref, ...), custom_call_target="tpu_custom_call" | custom-call | flops 7864320000 | bytes 2621440 | tf_op jit(solution)/shard_map/attend_fwd/pallas_call | solution.py:592
  101.0 7.8 %attend_fwd.5 = (bf16[512,640]{1,0:T(8,128)(2,1)S(1)}, f32[8,1,640]{2,1,0:T(1,128)S(1)}) custom-call(s32[1]{0:T(128)} %bitcast.1.place_ref, bf16[512,640]{1,0:T(8,128)(2,1)S(1)} %convolution_convert_fusion.16.qt_ref, bf16[1024,256]{1,0:T(8,128)(2,1)S(1)} %convolution_convert_fusion.27.pair_ref, s32[1,640]{1,0:T(1,128)S(1)} %constant_dynamic-slice_fusion.11.qseg_ref, ...), custom_call_target="tpu_custom_call" | custom-call | flops 786432000 | bytes 524288 | tf_op jit(solution)/shard_map/attend_fwd/pallas_call | solution.py:592
  115.1 28.6 %collective-permute-start.9 = (bf16[16,512]{1,0:T(8,128)(2,1)S(1)}, bf16[16,512]{1,0:T(8,128)(2,1)S(1)}, u32[]{:S(2)}, u32[]{:S(2)}) collective-permute-start(bf16[16,512]{1,0:T(8,128)(2,1)S(1)} %slice.327), channel_id=1, source_target_pairs={{0,1},{2,3},{4,5},{6,7},{8,9},{10,11},{12,13},{14,15},{16,17},{18,... | collective-permute-start | bytes 49160 | tf_op jit(solution)/shard_map/ppermute | solution.py:183
  146.3 24.1 %conv_fwd.1 = (bf16[640,512]{1,0:T(8,128)(2,1)S(1)}, bf16[640,512]{1,0:T(8,128)(2,1)S(1)}, bf16[640,1024]{1,0:T(8,128)(2,1)}, f32[640,512]{1,0:T(8,128)}, bf16[640,512]{1,0:T(8,128)(2,1)}) custom-call(f32[640,512]{1,0:T(8,128)} %copy-done.52, bf16[640,512]{1,0:T(8,128)(2,1)S(1)} %multiply_convert_fusion.3.a2_ref, ...), custom_call_target="tpu_custom_call" | custom-call | flops 6710886400 | bytes 5242880 | tf_op jit(solution)/shard_map/conv_fwd/pallas_call | solution.py:757
  177.9 18.7 %collective-permute-done.13 = bf16[128,4096]{0,1:T(8,128)(2,1)S(1)} collective-permute-done((bf16[128,4096]{0,1:T(8,128)(2,1)S(1)}, bf16[128,4096]{0,1:T(8,128)(2,1)S(1)}, u32[]{:S(2)}, u32[]{:S(2)}) %collective-permute-start.13) | collective-permute-done | bytes 1048608 | tf_op jit(solution)/shard_map/ppermute | solution.py:24
  206.3 3.5 collective-permute-done.12
  209.8 3.2 convolution_convert_fusion.pair_ref
  213.1 11.5 %attend_fwd.6 = (bf16[512,640]{1,0:T(8,128)(2,1)S(1)}, f32[8,1,640]{2,1,0:T(1,128)S(1)}) custom-call(s32[1]{0:T(128)} %bitcast.1.place_ref, bf16[512,640]{1,0:T(8,128)(2,1)S(1)} %convolution_convert_fusion.15.qt_ref, bf16[1024,1280]{1,0:T(8,128)(2,1)S(1)} %convolution_convert_fusion.pair_ref, s32[1,640]{1,0:T(1,128)S(1)} %constant_dynamic-slice_fusion.11.qseg_ref, ...), custom_call_target="tpu_custom_call" | custom-call | flops 3932160000 | bytes 2621440 | tf_op jit(solution)/shard_map/attend_fwd/pallas_call | solution.py:592
  230.8 7.5 %attend_fwd.7 = (bf16[512,640]{1,0:T(8,128)(2,1)S(1)}, f32[8,1,640]{2,1,0:T(1,128)S(1)}) custom-call(s32[1]{0:T(128)} %bitcast.1.place_ref, bf16[512,640]{1,0:T(8,128)(2,1)S(1)} %convolution_convert_fusion.14.qt_ref, bf16[1024,256]{1,0:T(8,128)(2,1)S(1)} %convolution_convert_fusion.26.pair_ref, s32[1,640]{1,0:T(1,128)S(1)} %constant_dynamic-slice_fusion.11.qseg_ref, ...), custom_call_target="tpu_custom_call" | custom-call | flops 786432000 | bytes 524288 | tf_op jit(solution)/shard_map/attend_fwd/pallas_call | solution.py:592
  249.0 2.8 fusion
  258.9 5.9 multiply_reduce_fusion
  267.6 7.3 %attend_bwd.4 = (bf16[512,640]{1,0:T(8,128)(2,1)S(1)}, bf16[1024,256]{1,0:T(8,128)(2,1)S(1)}) custom-call(s32[1]{0:T(128)} %bitcast.1.place_ref, bf16[512,640]{1,0:T(8,128)(2,1)S(1)} %copy-done.34, bf16[1024,256]{1,0:T(8,128)(2,1)S(1)} %copy-done.40, bf16[512,640]{1,0:T(8,128)(2,1)S(1)} %convolution_convert_fusion.13.gt_ref, ...), custom_call_target="tpu_custom_call" | custom-call | flops 1966080000 | bytes 1048576 | tf_op jit(solution)/shard_map/attend_bwd/pallas_call | solution.py:614
  281.3 14.2 %attend_bwd.5 = (bf16[512,640]{1,0:T(8,128)(2,1)S(1)}, bf16[1024,1280]{1,0:T(8,128)(2,1)S(1)}) custom-call(s32[1]{0:T(128)} %bitcast.1.place_ref, bf16[512,640]{1,0:T(8,128)(2,1)S(1)} %copy-done.28, bf16[1024,1280]{1,0:T(8,128)(2,1)} %copy-done.42, bf16[512,640]{1,0:T(8,128)(2,1)S(1)} %convolution_convert_fusion.12.gt_ref, ...), custom_call_target="tpu_custom_call" | custom-call | flops 9830400000 | bytes 5242880 | tf_op jit(solution)/shard_map/attend_bwd/pallas_call | solution.py:614
  297.7 3.3 convolution_convert_fusion.8
  308.9 3.6 convolution_convert_fusion.3
  312.6 28.6 %collective-permute-start.15 = (bf16[640,512]{1,0:T(8,128)(2,1)S(1)}, bf16[640,512]{1,0:T(8,128)(2,1)S(1)}, u32[]{:S(2)}, u32[]{:S(2)}) collective-permute-start(bf16[640,512]{1,0:T(8,128)(2,1)S(1)} %constant_dynamic-slice_fusion.2), channel_id=1, source_target_pairs={{0,1},{1,0},{2,3},{3,2},{4,5},{5,4},{6,7},{7,6},{8,9},{9,8},{10,11... | collective-permute-start | bytes 1966088 | tf_op jit(solution)/shard_map/ppermute | solution.py:148
  343.2 12.6 %collective-permute-done.17 = bf16[16,1024]{1,0:T(8,128)(2,1)S(1)} collective-permute-done((bf16[16,1024]{1,0:T(8,128)(2,1)S(1)}, bf16[16,1024]{1,0:T(8,128)(2,1)S(1)}, u32[]{:S(2)}, u32[]{:S(2)}) %collective-permute-start.17) | collective-permute-done | bytes 32800 | tf_op jit(solution)/shard_map/ppermute | solution.py:183
  374.3 37.9 %conv_bwd.1 = (f32[640,512]{1,0:T(8,128)S(1)}, bf16[512,2304]{1,0:T(8,128)(2,1)}, f32[11,512]{1,0:T(8,128)S(1)}, f32[7,512]{1,0:T(8,128)S(1)}, f32[7,1024]{1,0:T...) custom-call(f32[640,512]{1,0:T(8,128)} %copy-done.78, bf16[16,512]{1,0:T(8,128)(2,1)S(1)} %copy-done.24, ...), custom_call_target="tpu_custom_call" | custom-call | flops 13421772800 | bytes 13107200 | tf_op jit(solution)/shard_map/conv_bwd/pallas_call | solution.py:915
  413.5 3.3 constant_dynamic-update-slice_fusion.6
  418.4 3.8 reduce-scatter.9.cloned.1.call-done
  422.2 13.0 %reduce-scatter.7.cloned.1.call-done = bf16[16,4096]{1,0:T(8,128)(2,1)} async-done(((bf16[32,4096]{1,0:T(8,128)(2,1)}), bf16[16,4096]{1,0:T(8,128)(2,1)}) %reduce-scatter.7.cloned.1.call-update) | async-done | bytes 131088 | tf_op jit(solution)/shard_map/reduce_scatter | solution.py:173
  439.8 26.9 %attend_bwd.6 = (bf16[512,640]{1,0:T(8,128)(2,1)S(1)}, bf16[1024,1280]{1,0:T(8,128)(2,1)}) custom-call(s32[1]{0:T(128)} %bitcast.1.place_ref, bf16[512,640]{1,0:T(8,128)(2,1)S(1)} %copy-done.32, bf16[1024,1280]{1,0:T(8,128)(2,1)} %copy-done.43, bf16[512,640]{1,0:T(8,128)(2,1)S(1)} %convolution_convert_fusion.11.gt_ref, bf16[512,640]{1,0:T(8,128)(2,1)S(1)} %copy-done.4, ...), custom_call_target="tpu_custom_call" | custom-call | flops 19660800000 | bytes 5242880 | tf_op jit(solution)/shard_map/attend_bwd/pallas_call | solution.py:614
  466.7 3.5 convolution_convert_fusion.2
  470.3 27.1 %collective-permute-start.18 = (bf16[640,512]{1,0:T(8,128)(2,1)S(1)}, bf16[640,512]{1,0:T(8,128)(2,1)S(1)}, u32[]{:S(2)}, u32[]{:S(2)}) collective-permute-start(bf16[640,512]{1,0:T(8,128)(2,1)S(1)} %constant_dynamic-slice_fusion.1), channel_id=1, source_target_pairs={{0,1},{1,0},{2,3},{3,2},{4,5},{5,4},{6,7},{7,6},{8,9},{9,8},{10,11... | collective-permute-start | bytes 1966088 | tf_op jit(solution)/shard_map/ppermute | solution.py:148
  498.1 7.1 %attend_bwd.7 = (bf16[512,640]{1,0:T(8,128)(2,1)S(1)}, bf16[1024,256]{1,0:T(8,128)(2,1)S(1)}) custom-call(s32[1]{0:T(128)} %bitcast.1.place_ref, bf16[512,640]{1,0:T(8,128)(2,1)S(1)} %copy-done.36, bf16[1024,256]{1,0:T(8,128)(2,1)S(1)} %copy-done.38, bf16[512,640]{1,0:T(8,128)(2,1)S(1)} %convolution_convert_fusion.10.gt_ref, bf16[512,640]{1,0:T(8,128)(2,1)S(1)} %copy-done.6, ...), custom_call_target="tpu_custom_call" | custom-call | flops 1966080000 | bytes 1048576 | tf_op jit(solution)/shard_map/attend_bwd/pallas_call | solution.py:614
  515.3 5.2 fusion.12
  521.4 2.6 fusion.21
  525.5 6.9 %pad.25 = bf16[512,7168]{1,0:T(8,128)(2,1)} pad(bf16[512,6528]{1,0:T(8,128)(2,1)} %bitcast_dynamic-update-slice_fusion, bf16[]{:T(256)} %constant.64.clone.1), padding=0_0x0_640 | pad | bytes 14024706 | tf_op jit(solution)/shard_map/jit(_pad)/pad | solution.py:116
  532.4 82.0 %share_sum.1 = bf16[2,128,7168]{2,1,0:T(8,128)(2,1)S(1)} custom-call(bf16[2,2,128,7168]{3,2,1,0:T(8,128)(2,1)} %bitcast.182), custom_call_target="tpu_custom_call" | custom-call | tf_op jit(solution)/shard_map/share_sum/pallas_call | solution.py:564
  633.6 3.4 convert_bitcast_fusion
  (624 shorter events, 177.2 us)
Async XLA Ops:
  7.3 358.3 %reduce-scatter.5.cloned.1.call-start = ((), (), s32[]{:S(2)}) async-start(), calls=%async_computation.4 | async-start | bytes 4456448 | tf_op jit(solution)/shard_map/reduce_scatter | solution.py:169
  9.3 21.0 %collective-permute-start = (bf16[128,1536]{1,0:T(8,128)(2,1)}, bf16[128,1536]{1,0:T(8,128)(2,1)}, u32[]{:S(2)}, u32[]{:S(2)}) collective-permute-start(bf16[128,1536]{1,0:T(8,128)(2,1)} %constant_dynamic-slice_fusion.12), channel_id=1, source_target_pairs={{1,0},{0,1},{3,2},{2,3},{5,4},{4,5},{7,6},{6,7},{9,8},{8,9},{11,10... | collective-permute-start | bytes 1179656 | tf_op jit(solution)/shard_map/ppermute | solution.py:24
  12.2 24.3 %collective-permute-start.2 = (bf16[640,512]{1,0:T(8,128)(2,1)}, bf16[640,512]{1,0:T(8,128)(2,1)}, u32[]{:S(2)}, u32[]{:S(2)}) collective-permute-start(bf16[640,512]{1,0:T(8,128)(2,1)} %bitcast.185), channel_id=1, source_target_pairs={{1,0},{0,1},{3,2},{2,3},{5,4},{4,5},{7,6},{6,7},{9,8},{8,9},{11,10... | collective-permute-start | bytes 1966088 | tf_op jit(solution)/shard_map/ppermute | solution.py:24
  16.0 84.1 %copy-start.136 = (f32[640]{0:T(1024)}, f32[640]{0:T(1024)S(1)}, u32[]{:S(2)}) copy-start(f32[640]{0:T(1024)S(1)} %broadcast_multiply_fusion.13) | copy-start | bytes 7684
  17.0 263.3 %copy-start.15 = (s32[1,640]{1,0:T(1,128)}, s32[1,640]{1,0:T(1,128)S(1)}, u32[]{:S(2)}) copy-start(s32[1,640]{1,0:T(1,128)S(1)} %constant_dynamic-slice_fusion.11.qseg_ref) | copy-start | bytes 7684
  29.0 71.1 %copy-start.141 = (f32[640]{0:T(1024)}, f32[640]{0:T(1024)S(1)}, u32[]{:S(2)}) copy-start(f32[640]{0:T(1024)S(1)} %add_rsqrt_fusion.5) | copy-start | bytes 7684
  30.3 42.5 %collective-permute-start.6 = (bf16[128,1536]{1,0:T(8,128)(2,1)}, bf16[128,1536]{1,0:T(8,128)(2,1)}, u32[]{:S(2)}, u32[]{:S(2)}) collective-permute-start(bf16[128,1536]{1,0:T(8,128)(2,1)} %pad_maximum_fusion.3), channel_id=1, source_target_pairs={{1,0},{0,1},{3,2},{2,3},{5,4},{4,5},{7,6},{6,7},{9,8},{8,9},{11,10... | collective-permute-start | bytes 1179656 | tf_op jit(solution)/shard_map/ppermute | solution.py:24
  32.3 65.5 %collective-permute-start.8 = (bf16[128,512]{1,0:T(8,128)(2,1)}, bf16[128,512]{1,0:T(8,128)(2,1)S(1)}, u32[]{:S(2)}, u32[]{:S(2)}) collective-permute-start(bf16[128,512]{1,0:T(8,128)(2,1)} %bitcast.14), channel_id=1, source_target_pairs={{1,0},{0,1},{3,2},{2,3},{5,4},{4,5},{7,6},{6,7},{9,8},{8,9},{11,10... | collective-permute-start | bytes 393224 | tf_op jit(solution)/shard_map/ppermute | solution.py:24
  32.3 65.0 %collective-permute-start.4 = (bf16[128,3328]{1,0:T(8,128)(2,1)}, bf16[128,3328]{1,0:T(8,128)(2,1)}, u32[]{:S(2)}, u32[]{:S(2)}) collective-permute-start(bf16[128,3328]{1,0:T(8,128)(2,1)} %pad_maximum_fusion.2), channel_id=1, source_target_pairs={{1,0},{0,1},{3,2},{2,3},{5,4},{4,5},{7,6},{6,7},{9,8},{8,9},{11,10... | collective-permute-start | bytes 2555912 | tf_op jit(solution)/shard_map/ppermute | solution.py:24
  34.3 32.1 %collective-permute-start.1 = (bf16[128,1536]{1,0:T(8,128)(2,1)}, bf16[128,1536]{1,0:T(8,128)(2,1)}, u32[]{:S(2)}, u32[]{:S(2)}) collective-permute-start(bf16[128,1536]{1,0:T(8,128)(2,1)} %collective-permute-done), channel_id=1, source_target_pairs={{0,2},{2,0},{4,6},{6,4},{8,10},{10,8},{12,14},{14,12},{16,18},{18,... | collective-permute-start | bytes 1179656 | tf_op jit(solution)/shard_map/ppermute | solution.py:28
  38.3 32.4 %copy-start.57 = (bf16[1280,512]{1,0:T(8,128)(2,1)}, bf16[1280,512]{1,0:T(8,128)(2,1)S(1)}, u32[]{:S(2)}) copy-start(bf16[1280,512]{1,0:T(8,128)(2,1)S(1)} %get-tuple-element.209) | copy-start | bytes 3932164
  38.3 27.2 %collective-permute-start.3 = (bf16[80,128]{1,0:T(8,128)(2,1)S(1)}, bf16[80,128]{1,0:T(8,128)(2,1)S(1)}, u32[]{:S(2)}, u32[]{:S(2)}) collective-permute-start(bf16[80,128]{1,0:T(8,128)(2,1)S(1)} %pad_bitcast_fusion), channel_id=1, source_target_pairs={{1,0},{0,1},{3,2},{2,3},{5,4},{4,5},{7,6},{6,7},{9,8},{8,9},{11,10... | collective-permute-start | bytes 61448 | tf_op jit(solution)/shard_map/ppermute | solution.py:24
  65.7 80.6 %copy-start.13 = (f32[1,1024]{1,0:T(1,128)}, f32[1,1024]{1,0:T(1,128)S(1)}, u32[]{:S(2)}) copy-start(f32[1,1024]{1,0:T(1,128)S(1)} %fusion.63.mgain_ref) | copy-start | bytes 12292
  66.3 33.7 %copy-start.144 = (f32[1,512]{1,0:T(1,128)}, f32[1,512]{1,0:T(1,128)S(1)}, u32[]{:S(2)}) copy-start(f32[1,512]{1,0:T(1,128)S(1)} %get-tuple-element.241) | copy-start | bytes 6148
  72.8 24.3 %collective-permute-start.7 = (bf16[128,1536]{1,0:T(8,128)(2,1)}, bf16[128,1536]{1,0:T(8,128)(2,1)S(1)}, u32[]{:S(2)}, u32[]{:S(2)}) collective-permute-start(bf16[128,1536]{1,0:T(8,128)(2,1)} %collective-permute-done.6), channel_id=1, source_target_pairs={{0,2},{2,0},{4,6},{6,4},{8,10},{10,8},{12,14},{14,12},{16,18},{18,... | collective-permute-start | bytes 1179656 | tf_op jit(solution)/shard_map/ppermute | solution.py:28
  97.3 13.9 %collective-permute-start.5 = (bf16[128,3328]{1,0:T(8,128)(2,1)}, bf16[128,3328]{1,0:T(8,128)(2,1)S(1)}, u32[]{:S(2)}, u32[]{:S(2)}) collective-permute-start(bf16[128,3328]{1,0:T(8,128)(2,1)} %collective-permute-done.4), channel_id=1, source_target_pairs={{0,2},{2,0},{4,6},{6,4},{8,10},{10,8},{12,14},{14,12},{16,18},{18,... | collective-permute-start | bytes 2555912 | tf_op jit(solution)/shard_map/ppermute | solution.py:28
  115.1 31.1 %collective-permute-start.9 = (bf16[16,512]{1,0:T(8,128)(2,1)S(1)}, bf16[16,512]{1,0:T(8,128)(2,1)S(1)}, u32[]{:S(2)}, u32[]{:S(2)}) collective-permute-start(bf16[16,512]{1,0:T(8,128)(2,1)S(1)} %slice.327), channel_id=1, source_target_pairs={{0,1},{2,3},{4,5},{6,7},{8,9},{10,11},{12,13},{14,15},{16,17},{18,... | collective-permute-start | bytes 49160 | tf_op jit(solution)/shard_map/ppermute | solution.py:183
  146.3 26.3 %collective-permute-start.10 = (bf16[128,4096]{1,0:T(8,128)(2,1)S(1)}, bf16[128,4096]{1,0:T(8,128)(2,1)}, u32[]{:S(2)}, u32[]{:S(2)}) collective-permute-start(bf16[128,4096]{1,0:T(8,128)(2,1)S(1)} %copy-done.119), channel_id=1, source_target_pairs={{1,0},{0,1},{3,2},{2,3},{5,4},{4,5},{7,6},{6,7},{9,8},{8,9},{11,10... | collective-permute-start | bytes 3145736 | tf_op jit(solution)/shard_map/ppermute | solution.py:24
  170.5 26.1 %collective-permute-start.13 = (bf16[128,4096]{0,1:T(8,128)(2,1)S(1)}, bf16[128,4096]{0,1:T(8,128)(2,1)S(1)}, u32[]{:S(2)}, u32[]{:S(2)}) collective-permute-start(bf16[128,4096]{0,1:T(8,128)(2,1)S(1)} %copy-done.90), channel_id=1, source_target_pairs={{1,0},{0,1},{3,2},{2,3},{5,4},{4,5},{7,6},{6,7},{9,8},{8,9},{11,10... | collective-permute-start | bytes 3145736 | tf_op jit(solution)/shard_map/ppermute | solution.py:24
  172.5 27.4 %collective-permute-start.11 = (bf16[128,4096]{1,0:T(8,128)(2,1)}, bf16[128,4096]{1,0:T(8,128)(2,1)}, u32[]{:S(2)}, u32[]{:S(2)}) collective-permute-start(bf16[128,4096]{1,0:T(8,128)(2,1)} %collective-permute-done.10), channel_id=1, source_target_pairs={{0,2},{2,0},{4,6},{6,4},{8,10},{10,8},{12,14},{14,12},{16,18},{18,... | collective-permute-start | bytes 3145736 | tf_op jit(solution)/shard_map/ppermute | solution.py:28
  172.5 37.3 %collective-permute-start.12 = (bf16[640,512]{1,0:T(8,128)(2,1)}, bf16[640,512]{1,0:T(8,128)(2,1)}, u32[]{:S(2)}, u32[]{:S(2)}) collective-permute-start(bf16[640,512]{1,0:T(8,128)(2,1)} %get-tuple-element.71), channel_id=1, source_target_pairs={{1,0},{0,1},{3,2},{2,3},{5,4},{4,5},{7,6},{6,7},{9,8},{8,9},{11,10... | collective-permute-start | bytes 1966088 | tf_op jit(solution)/shard_map/ppermute | solution.py:24
  199.9 39.5 %collective-permute-start.14 = (bf16[128,4096]{0,1:T(8,128)(2,1)}, bf16[128,4096]{0,1:T(8,128)(2,1)S(1)}, u32[]{:S(2)}, u32[]{:S(2)}) collective-permute-start(bf16[128,4096]{0,1:T(8,128)(2,1)} %copy-done.91), channel_id=1, source_target_pairs={{0,2},{2,0},{4,6},{6,4},{8,10},{10,8},{12,14},{14,12},{16,18},{18,... | collective-permute-start | bytes 3145736 | tf_op jit(solution)/shard_map/ppermute | solution.py:28
  258.8 163.4 %reduce-scatter.9.cloned.1.call-start = ((), (), s32[]{:S(2)}) async-start(), calls=%async_computation.6 | async-start | bytes 4456448 | tf_op jit(solution)/shard_map/reduce_scatter | solution.py:169
  304.3 130.9 %reduce-scatter.7.cloned.1.call-start = ((), (), s32[]{:S(2)}) async-start(), calls=%async_computation.5 | async-start | bytes 393216 | tf_op jit(solution)/shard_map/reduce_scatter | solution.py:173
  312.6 43.9 %collective-permute-start.15 = (bf16[640,512]{1,0:T(8,128)(2,1)S(1)}, bf16[640,512]{1,0:T(8,128)(2,1)S(1)}, u32[]{:S(2)}, u32[]{:S(2)}) collective-permute-start(bf16[640,512]{1,0:T(8,128)(2,1)S(1)} %constant_dynamic-slice_fusion.2), channel_id=1, source_target_pairs={{0,1},{1,0},{2,3},{3,2},{4,5},{5,4},{6,7},{7,6},{8,9},{9,8},{10,11... | collective-permute-start | bytes 1966088 | tf_op jit(solution)/shard_map/ppermute | solution.py:148
  341.2 14.6 %collective-permute-start.17 = (bf16[16,1024]{1,0:T(8,128)(2,1)S(1)}, bf16[16,1024]{1,0:T(8,128)(2,1)S(1)}, u32[]{:S(2)}, u32[]{:S(2)}) collective-permute-start(bf16[16,1024]{1,0:T(8,128)(2,1)S(1)} %pad_maximum_fusion.4), channel_id=1, source_target_pairs={{1,0},{3,2},{5,4},{7,6},{9,8},{11,10},{13,12},{15,14},{17,16},{19,... | collective-permute-start | bytes 98312 | tf_op jit(solution)/shard_map/ppermute | solution.py:183
  359.4 6.2 collective-permute-start.16
  413.5 101.8 %reduce-scatter.11.cloned.1.call-start = ((), (), s32[]{:S(2)}) async-start(), calls=%async_computation.7 | async-start | bytes 393216 | tf_op jit(solution)/shard_map/reduce_scatter | solution.py:173
  435.2 198.4 %all-gather.5.cloned.1.call-start = ((), (), s32[]{:S(2)}) async-start(), calls=%async_computation.9 | async-start | bytes 2228224 | tf_op jit(solution)/shard_map/all_gather | solution.py:177
  438.5 200.3 %all-gather.3.cloned.1.call-start = ((), (), s32[]{:S(2)}) async-start(), calls=%async_computation.8 | async-start | bytes 2228224 | tf_op jit(solution)/shard_map/all_gather | solution.py:177
  470.3 43.4 %collective-permute-start.18 = (bf16[640,512]{1,0:T(8,128)(2,1)S(1)}, bf16[640,512]{1,0:T(8,128)(2,1)S(1)}, u32[]{:S(2)}, u32[]{:S(2)}) collective-permute-start(bf16[640,512]{1,0:T(8,128)(2,1)S(1)} %constant_dynamic-slice_fusion.1), channel_id=1, source_target_pairs={{0,1},{1,0},{2,3},{3,2},{4,5},{5,4},{6,7},{7,6},{8,9},{9,8},{10,11... | collective-permute-start | bytes 1966088 | tf_op jit(solution)/shard_map/ppermute | solution.py:148
  507.1 13.5 %collective-permute-start.19 = (bf16[128,512]{1,0:T(8,128)(2,1)S(1)}, bf16[128,512]{1,0:T(8,128)(2,1)S(1)}, u32[]{:S(2)}, u32[]{:S(2)}) collective-permute-start(bf16[128,512]{1,0:T(8,128)(2,1)S(1)} %constant_dynamic-slice_fusion), channel_id=1, source_target_pairs={{0,1},{1,0},{2,3},{3,2},{4,5},{5,4},{6,7},{7,6},{8,9},{9,8},{10,11... | collective-permute-start | bytes 393224 | tf_op jit(solution)/shard_map/ppermute | solution.py:148
  (165 other events, 1069.9 us)
Sparse Core Ops, SparseCore 0:
  258.9 87.1 reduce-scatter.4
  350.4 71.7 reduce-scatter.8
  424.4 10.7 reduce-scatter.6
  437.4 11.6 reduce-scatter.10
  451.1 41.5 all-gather.4
  515.4 42.5 all-gather.2
